TPU v7x, 512 devices: a whole 4x8x8 slice. The times are simulated.
512 devices in a mesh: gx: 16 (over z_lo, y), gy: 32 (over z_hi, x, core).
Axes of the slice: x: 4, y: 8, z: 8 (z_hi: 4, z_lo: 2; z = z_hi * 2 + z_lo), core: 2. Of those that a mesh axis runs over, the one named last changes fastest.
Arguments:
- positions: float32 [16, 32, 3, 384], P('gx', 'gy'), may hold values from 0 to 36, as said below
- features: bfloat16 [16, 32, 128, 384], P('gx', 'gy'), may hold values from -12 to 12
- nbr_tiles: int32 [16, 32, 3, 32], P('gx', 'gy'), may hold values from 0 to 27, as said below
- kvec_index: int32 [3, 4096], replicated, may hold values from -8 to 8, as said below
- weight_charge: bfloat16 [16, 128], replicated, may hold values from -0.5 to 0.5
- weight_pair: bfloat16 [16, 128], replicated, may hold values from -0.5 to 0.5
Outputs:
- energy: float32 [], replicated
- forces: float32 [16, 32, 3, 384], P('gx', 'gy')
Inputs may be any that keep to these rules, and one draw needn't show every extreme that they name: `nbr_tiles`: an entry below 27 names a tile of the neighbourhood, each at most once in a row; 27 marks an empty slot. `kvec_index`: the third component is 1 or more. `positions`: atoms of block b of a column have z between 12 b and 12 (b + 1); x and y lie between 0 and 10.
All inputs are finite; a program needn't handle non-finite values.
Results may differ from a plain program's by a relative error of at most 0.0055.
Values sent between devices are 32-bit elements; how exact they have to be, the bound alone decides.
A program may use at most 64 MiB of HBM per device.

v0:
```python
import math

import jax
import jax.numpy as jnp
from jax import lax
from jax.sharding import PartitionSpec as P

column_width = 10.0
slab_depth = 12.0
cutoff = 5.0
smear = 1.5
pair_scale = 0.25


def with_halo(block, sides, width):
    for axis, dim in sides:
        count = lax.axis_size(axis)
        forward = [(i, i + 1) for i in range(count - 1)]
        forward.append((count - 1, 0))
        backward = [(target, source) for source, target in forward]
        low = lax.ppermute(
            lax.slice_in_dim(block, block.shape[dim] - width, None, axis=dim), axis, forward
        )
        high = lax.ppermute(lax.slice_in_dim(block, 0, width, axis=dim), axis, backward)
        block = jnp.concatenate([low, block, high], axis=dim)
    return block


def block_terms(own_pos, own_feat, tile_pos, tile_feat, row, block, nblk, depth):
    tile = own_pos.shape[1]
    picked_pos = jnp.take(tile_pos, row, axis=0)
    picked_feat = jnp.take(tile_feat, row, axis=0)
    coupling = jnp.einsum("ci,ncj->nij", own_feat, picked_feat, precision=lax.Precision.HIGHEST)
    delta = own_pos[None, :, :, None] - picked_pos[:, :, None, :]
    along_z = delta[:, 2]
    along_z = along_z - depth * jnp.floor(along_z / depth + 0.5)
    dist = (delta[:, 0] * delta[:, 0] + delta[:, 1] * delta[:, 1] + along_z * along_z) / (
        cutoff * cutoff
    )
    weight = jnp.maximum(1.0 - dist, 0.0)
    valid = (row < 9 * nblk).astype(jnp.float32)
    same = (row == 4 * nblk + block).astype(jnp.float32)
    ident = jnp.eye(tile, dtype=jnp.float32)
    mask = valid[:, None, None] * (1.0 - same[:, None, None] * ident[None])
    coupling = coupling * mask
    energy = 0.5 * pair_scale * jnp.sum(coupling * weight * weight)
    scaled = coupling * weight
    force_x = jnp.sum(scaled * delta[:, 0], axis=(0, 2))
    force_y = jnp.sum(scaled * delta[:, 1], axis=(0, 2))
    force_z = jnp.sum(scaled * along_z, axis=(0, 2))
    force = 4.0 * pair_scale / (cutoff * cutoff) * jnp.stack([force_x, force_y, force_z])
    return (energy, force)


def make_tiles(hood, nblk, tile, with_shift):
    if with_shift:
        offset = (jnp.arange(3).astype(jnp.float32) - 1.0) * column_width
        xs = hood[:, :, 0] + offset[:, None, None]
        ys = hood[:, :, 1] + offset[None, :, None]
        hood = jnp.stack([xs, ys, hood[:, :, 2]], axis=2)
    chans = hood.shape[2]
    tiles = hood.reshape(9, chans, nblk, tile).transpose(0, 2, 1, 3).reshape(9 * nblk, chans, tile)
    return jnp.concatenate([tiles, jnp.zeros((1, chans, tile), jnp.float32)], axis=0)


def pair_terms(pos_col, feat_col, hood_pos, hood_feat, rows):
    tile = 128
    atoms = pos_col.shape[1]
    nblk = atoms // tile
    depth = nblk * slab_depth
    tile_pos = make_tiles(hood_pos, nblk, tile, True)
    tile_feat = make_tiles(hood_feat, nblk, tile, False)
    own_pos = pos_col.reshape(3, nblk, tile).transpose(1, 0, 2)
    own_feat = feat_col.reshape(feat_col.shape[0], nblk, tile).transpose(1, 0, 2)

    def one_block(items):
        block, opos, ofeat, row = items
        return block_terms(opos, ofeat, tile_pos, tile_feat, row, block, nblk, depth)

    energies, forces = lax.map(one_block, (jnp.arange(nblk), own_pos, own_feat, rows))
    return (jnp.sum(energies), forces.transpose(1, 0, 2).reshape(3, atoms))


def trig(glob, kvec):
    theta = lax.dot_general(
        glob,
        kvec,
        (((0,), (0,)), ((), ())),
        precision=lax.Precision.HIGHEST,
        preferred_element_type=jnp.float32,
    )
    return (jnp.cos(theta).astype(jnp.bfloat16), jnp.sin(theta).astype(jnp.bfloat16))


def on_device(positions, features, nbr_tiles, kvec_index, weight_charge, weight_pair):
    cols_x = lax.axis_size("gx")
    cols_y = lax.axis_size("gy")
    atoms = positions.shape[3]
    nblk = atoms // 128
    ntot = cols_x * cols_y * atoms
    kcount = kvec_index.shape[1]
    norm = 1.0 / math.sqrt(ntot * kcount)
    local_pos = positions[0, 0]
    feat = features[0, 0]
    charges = jnp.dot(weight_charge, feat, preferred_element_type=jnp.float32).astype(jnp.bfloat16)
    pair_feat = jnp.dot(weight_pair, feat, preferred_element_type=jnp.float32)
    corner_x = lax.axis_index("gx").astype(jnp.float32) * column_width
    corner_y = lax.axis_index("gy").astype(jnp.float32) * column_width
    glob = jnp.stack([local_pos[0] + corner_x, local_pos[1] + corner_y, local_pos[2]])
    box = jnp.array([cols_x * column_width, cols_y * column_width, nblk * slab_depth], jnp.float32)
    kvec = 2.0 * math.pi * kvec_index.astype(jnp.float32) / box[:, None]
    ksq = jnp.sum(kvec * kvec, axis=0)
    green = 2.0 * jnp.exp(-0.5 * smear * smear * ksq) / ksq * norm
    width = min(512, kcount)
    nparts = kcount // width
    kblocks = kvec.reshape(3, nparts, width).transpose(1, 0, 2)

    def forward(kblk):
        cs, sn = trig(glob, kblk)
        return jnp.stack(
            [
                jnp.dot(charges, cs, preferred_element_type=jnp.float32),
                jnp.dot(charges, sn, preferred_element_type=jnp.float32),
            ]
        )

    partial_value = lax.map(forward, kblocks)
    partial_value = partial_value.transpose(1, 2, 0, 3).reshape(2, charges.shape[0], kcount)
    factors = lax.psum(partial_value, ("gx", "gy"))
    block_feat = pair_feat[None, None]
    hood_pos, hood_feat = (
        with_halo(positions, (("gx", 0), ("gy", 1)), 1),
        with_halo(block_feat, (("gx", 0), ("gy", 1)), 1),
    )
    e_local, force_pair = pair_terms(local_pos, pair_feat, hood_pos, hood_feat, nbr_tiles[0, 0])
    e_pair = lax.psum(e_local, ("gx", "gy"))
    re, im = (factors[0], factors[1])
    e_long = jnp.sum(green[None, :] * (re * re + im * im))
    pf = (2.0 * green[None, :] * re).astype(jnp.bfloat16)
    qf = (2.0 * green[None, :] * im).astype(jnp.bfloat16)
    pblocks = pf.reshape(pf.shape[0], nparts, width).transpose(1, 0, 2)
    qblocks = qf.reshape(qf.shape[0], nparts, width).transpose(1, 0, 2)

    def backward(total, items):
        kblk, pblk, qblk = items
        cs, sn = trig(glob, kblk)
        dims = (((0,), (0,)), ((), ()))
        vc = lax.dot_general(charges, qblk, dims, preferred_element_type=jnp.float32)
        vs = lax.dot_general(charges, pblk, dims, preferred_element_type=jnp.float32)
        wmat = cs.astype(jnp.float32) * vc - sn.astype(jnp.float32) * vs
        grad = lax.dot_general(
            kblk,
            wmat,
            (((1,), (1,)), ((), ())),
            precision=lax.Precision.HIGHEST,
            preferred_element_type=jnp.float32,
        )
        return (total + grad, None)

    grad_long, _ = lax.scan(
        backward, jnp.zeros((3, atoms), jnp.float32), (kblocks, pblocks, qblocks)
    )
    energy = (e_long + e_pair) / ntot
    forces = (force_pair - grad_long)[None, None]
    return (energy, forces)


def solution(mesh):
    in_specs = (
        P("gx", "gy", None, None),
        P("gx", "gy", None, None),
        P("gx", "gy", None, None),
        P(),
        P(),
        P(),
    )
    out_specs = (P(), P("gx", "gy", None, None))
    return jax.shard_map(
        on_device, mesh=mesh, in_specs=in_specs, out_specs=out_specs, check_vma=False
    )
```

profile of v0, /device:TPU:1, one launch (start us, length us, event | category | flops | bytes accessed | tf_op | source)
XLA Modules:
  0.0 429.5 jit_solution(18117224486216164463)
XLA Ops:
  7.2 4.0 collective-permute-start.4
  11.3 5.6 %collective-permute-start.5 = (f32[1,1,3,384]{3,1,2,0:T(1,128)}, f32[1,1,3,384]{3,1,2,0:T(1,128)S(1)}, u32[]{:S(2)}, u32[]{:S(2)}) collective-permute-start(f32[1,1,3,384]{3,1,2,0:T(1,128)} %param.13), channel_id=1, source_target_pairs={{32,0},{64,32},{96,64},{128,96},{160,128},{192,160},{224,192},{256... | collective-permute-start | bytes 13832 | tf_op jit(solution)/shard_map/ppermute | solution.py:24
  17.7 3.4 collective-permute-start.1
  25.6 57.8 %while.33 = (s32[]{:T(128)}, f32[8,2,16,512]{3,2,1,0:T(8,128)S(1)}, f32[8,3,512]{2,1,0:T(4,128)S(1)}, f32[3,384]{1,0:T(4,128)S(1)}, bf16[16,384]{1,0:T(8,128)(2,1)S(1)}, /*index=5*/s32[]{:T(128)}) while((s32[]{:T(128)}, f32[8,2,16,512]{3,2,1,0:T(8,128)S(1)}, f32[8,3,512]{2,1,0:T(4,128)S(1)}, f32[3,384]{1,0:T(4,128)S(1)}, ...), condition=%wide.region_2.3_spmd, body=%wide.region_1.2_spmd.sunk | while | flops 20070400 | bytes 2594901 | solution.py:127
  26.7 3.0 convolution_bitcast_fusion.5
  29.7 3.0 convolution_bitcast_fusion.4
  34.0 3.0 convolution_bitcast_fusion.5
  37.0 3.0 convolution_bitcast_fusion.4
  41.2 3.0 convolution_bitcast_fusion.5
  44.2 3.0 convolution_bitcast_fusion.4
  48.4 3.0 convolution_bitcast_fusion.5
  51.4 3.0 convolution_bitcast_fusion.4
  55.6 3.0 convolution_bitcast_fusion.5
  58.6 3.0 convolution_bitcast_fusion.4
  62.9 3.0 convolution_bitcast_fusion.5
  65.9 3.0 convolution_bitcast_fusion.4
  70.1 3.0 convolution_bitcast_fusion.5
  73.1 3.0 convolution_bitcast_fusion.4
  77.3 3.0 convolution_bitcast_fusion.5
  80.3 3.0 convolution_bitcast_fusion.4
  84.4 7.6 %collective-permute-start.7 = (f32[3,1,3,384]{3,1,2,0:T(1,128)S(1)}, f32[3,1,3,384]{3,1,2,0:T(1,128)S(1)}, u32[]{:S(2)}, u32[]{:S(2)}) collective-permute-start(f32[3,1,3,384]{3,1,2,0:T(1,128)S(1)} %constant_dynamic-update-slice_fusion), channel_id=1, source_target_pairs={{1,0},{2,1},{3,2},{4,3},{5,4},{6,5},{7,6},{8,7},{9,8},{10,9},{11,1... | collective-permute-start | bytes 41480 | tf_op jit(solution)/shard_map/ppermute | solution.py:24
  94.1 5.3 %collective-permute-done.6 = f32[3,1,3,384]{3,1,2,0:T(1,128)S(1)} collective-permute-done((f32[3,1,3,384]{3,1,2,0:T(1,128)S(1)}, f32[3,1,3,384]{3,1,2,0:T(1,128)S(1)}, u32[]{:S(2)}, u32[]{:S(2)}) %collective-permute-start.6) | collective-permute-done | bytes 13856 | tf_op jit(solution)/shard_map/ppermute | solution.py:21
  99.6 8.6 %collective-permute-start.3 = (f32[3,1,16,384]{3,2,1,0:T(8,128)S(1)}, f32[3,1,16,384]{3,2,1,0:T(8,128)S(1)}, u32[]{:S(2)}, u32[]{:S(2)}) collective-permute-start(f32[3,1,16,384]{3,2,1,0:T(8,128)S(1)} %pad_maximum_fusion.1), channel_id=1, source_target_pairs={{1,0},{2,1},{3,2},{4,3},{5,4},{6,5},{7,6},{8,7},{9,8},{10,9},{11,1... | collective-permute-start | bytes 221192 | tf_op jit(solution)/shard_map/ppermute | solution.py:24
  111.6 32.9 %while.34 = (s32[]{:T(128)}, f32[3]{0:T(128)S(1)}, f32[3,3,128]{2,1,0:T(4,128)S(1)}, s32[3,32]{1,0:T(4,128)S(1)}, f32[28,16,128]{2,1,0:T(8,128)S(1)}, /*index=5*...) while((s32[]{:T(128)}, f32[3]{0:T(128)S(1)}, ...), condition=%wide.region_10.11_spmd, body=%wide.region_5.10_spmd.sunk | while | flops 115980448 | bytes 13887781 | solution.py:80
  116.3 5.5 %multiply_reduce_fusion.6 = (f32[128]{0:T(128)S(1)}, f32[128]{0:T(128)S(1)}, f32[128]{0:T(128)S(1)}, f32[]{:T(128)}) fusion(f32[32,3,128,128]{2,3,0,1:T(8,128)S(1)} %broadcast_subtract_fusion.2, f32[128,128]{0,1:T(8,128)S(1)} %fusion.72, f32[32]{0:T(128)S(1)} %get-tuple-element.370, f32[32]{0:T(128)S(1)} %get-tuple-element.371, ...), kind=kOutput, calls=%fused_computation.20.clone.1 | convolution fusion | flops 114359936 | bytes 6629156 | tf_op jit(solution)/shard_map/while/body/eval_jaxpr/ci,ncj->nij/dot_general | solution.py:33
  127.2 5.5 %multiply_reduce_fusion.6 = (f32[128]{0:T(128)S(1)}, f32[128]{0:T(128)S(1)}, f32[128]{0:T(128)S(1)}, f32[]{:T(128)}) fusion(f32[32,3,128,128]{2,3,0,1:T(8,128)S(1)} %broadcast_subtract_fusion.2, f32[128,128]{0,1:T(8,128)S(1)} %fusion.72, f32[32]{0:T(128)S(1)} %get-tuple-element.370, f32[32]{0:T(128)S(1)} %get-tuple-element.371, ...), kind=kOutput, calls=%fused_computation.20.clone.1 | convolution fusion | flops 114359936 | bytes 6629156 | tf_op jit(solution)/shard_map/while/body/eval_jaxpr/ci,ncj->nij/dot_general | solution.py:33
  138.2 5.5 %multiply_reduce_fusion.6 = (f32[128]{0:T(128)S(1)}, f32[128]{0:T(128)S(1)}, f32[128]{0:T(128)S(1)}, f32[]{:T(128)}) fusion(f32[32,3,128,128]{2,3,0,1:T(8,128)S(1)} %broadcast_subtract_fusion.2, f32[128,128]{0,1:T(8,128)S(1)} %fusion.72, f32[32]{0:T(128)S(1)} %get-tuple-element.370, f32[32]{0:T(128)S(1)} %get-tuple-element.371, ...), kind=kOutput, calls=%fused_computation.20.clone.1 | convolution fusion | flops 114359936 | bytes 6629156 | tf_op jit(solution)/shard_map/while/body/eval_jaxpr/ci,ncj->nij/dot_general | solution.py:33
  145.1 102.0 %psum.15 = f32[]{:T(128)} all-reduce(f32[]{:T(128)} %reduce_sum.67), channel_id=1, replica_groups=mesh['gx'=16,'gy'=32] {'gx','gy'}, use_global_device_ids=true, to_apply=%region_12.13 | all-reduce | flops 1 | bytes 8 | tf_op jit(solution)/shard_map/psum | solution.py:136
  247.1 110.7 %all-reduce.4.cloned.1.call-done = f32[2,16,4096]{2,1,0:T(8,128)} async-done(((f32[2,16,4096]{2,1,0:T(8,128)}), f32[2,16,4096]{2,1,0:T(8,128)}) %all-reduce.4.cloned.1.call-update) | async-done | bytes 524304 | tf_op jit(solution)/shard_map/psum | solution.py:129
  359.4 59.5 %while.35 = (s32[]{:T(128)}, f32[3,384]{1,0:T(4,128)S(1)}, f32[8,3,512]{2,1,0:T(4,128)S(1)}, f32[3,384]{1,0:T(4,128)S(1)}, bf16[8,16,512]{2,1,0:T(8,128)(2,1)S(1...) while((s32[]{:T(128)}, f32[3,384]{1,0:T(4,128)S(1)}, ...), condition=%wide.region_14.15_spmd.clone, body=%wide.region_13.14_spmd.clone.sunk | while | flops 28117248 | bytes 5595775 | solution.py:160
  378.3 2.9 fusion.83
  385.7 2.9 fusion.83
  (158 shorter events, 89.5 us)
Async XLA Ops:
  7.2 9.7 %copy-start = (bf16[1,1,128,384]{3,2,1,0:T(8,128)(2,1)S(1)}, bf16[1,1,128,384]{3,2,1,0:T(8,128)(2,1)}, u32[]{:S(2)}) copy-start(bf16[1,1,128,384]{3,2,1,0:T(8,128)(2,1)} %param.14) | copy-start | bytes 294916
  7.2 350.6 %all-reduce.4.cloned.1.call-start = ((), (), s32[]{:S(2)}) async-start(), calls=%async_computation | async-start | bytes 1048576 | tf_op jit(solution)/shard_map/psum | solution.py:129
  7.2 77.1 %collective-permute-start.4 = (f32[1,1,3,384]{3,1,2,0:T(1,128)}, f32[1,1,3,384]{3,1,2,0:T(1,128)S(1)}, u32[]{:S(2)}, u32[]{:S(2)}) collective-permute-start(f32[1,1,3,384]{3,1,2,0:T(1,128)} %param.13), channel_id=1, source_target_pairs={{0,32},{32,64},{64,96},{96,128},{128,160},{160,192},{192,224},{224... | collective-permute-start | bytes 13832 | tf_op jit(solution)/shard_map/ppermute | solution.py:21
  11.3 73.1 %collective-permute-start.5 = (f32[1,1,3,384]{3,1,2,0:T(1,128)}, f32[1,1,3,384]{3,1,2,0:T(1,128)S(1)}, u32[]{:S(2)}, u32[]{:S(2)}) collective-permute-start(f32[1,1,3,384]{3,1,2,0:T(1,128)} %param.13), channel_id=1, source_target_pairs={{32,0},{64,32},{96,64},{128,96},{160,128},{192,160},{224,192},{256... | collective-permute-start | bytes 13832 | tf_op jit(solution)/shard_map/ppermute | solution.py:24
  17.7 81.8 %collective-permute-start.1 = (f32[1,1,16,384]{3,2,1,0:T(8,128)S(1)}, f32[1,1,16,384]{3,2,1,0:T(8,128)S(1)}, u32[]{:S(2)}, u32[]{:S(2)}) collective-permute-start(f32[1,1,16,384]{3,2,1,0:T(8,128)S(1)} %bitcast.213), channel_id=1, source_target_pairs={{32,0},{64,32},{96,64},{128,96},{160,128},{192,160},{224,192},{256... | collective-permute-start | bytes 73736 | tf_op jit(solution)/shard_map/ppermute | solution.py:24
  21.1 78.4 %collective-permute-start = (f32[1,1,16,384]{3,2,1,0:T(8,128)S(1)}, f32[1,1,16,384]{3,2,1,0:T(8,128)S(1)}, u32[]{:S(2)}, u32[]{:S(2)}) collective-permute-start(f32[1,1,16,384]{3,2,1,0:T(8,128)S(1)} %bitcast.214), channel_id=1, source_target_pairs={{0,32},{32,64},{64,96},{96,128},{128,160},{160,192},{192,224},{224... | collective-permute-start | bytes 73736 | tf_op jit(solution)/shard_map/ppermute | solution.py:21
  25.6 58.8 %copy-start.2 = (f32[1,1,3,384]{3,1,2,0:T(1,128)S(1)}, f32[1,1,3,384]{3,1,2,0:T(1,128)}, u32[]{:S(2)}) copy-start(f32[1,1,3,384]{3,1,2,0:T(1,128)} %param.13) | copy-start | bytes 13828
  25.6 68.5 %copy-start.3 = (s32[1,1,3,32]{3,1,2,0:T(1,128)S(1)}, s32[1,1,3,32]{3,1,2,0:T(1,128)}, u32[]{:S(2)}) copy-start(s32[1,1,3,32]{3,1,2,0:T(1,128)} %param.15) | copy-start | bytes 1156
  84.4 9.7 %collective-permute-start.7 = (f32[3,1,3,384]{3,1,2,0:T(1,128)S(1)}, f32[3,1,3,384]{3,1,2,0:T(1,128)S(1)}, u32[]{:S(2)}, u32[]{:S(2)}) collective-permute-start(f32[3,1,3,384]{3,1,2,0:T(1,128)S(1)} %constant_dynamic-update-slice_fusion), channel_id=1, source_target_pairs={{1,0},{2,1},{3,2},{4,3},{5,4},{6,5},{7,6},{8,7},{9,8},{10,9},{11,1... | collective-permute-start | bytes 41480 | tf_op jit(solution)/shard_map/ppermute | solution.py:24
  92.1 7.3 %collective-permute-start.6 = (f32[3,1,3,384]{3,1,2,0:T(1,128)S(1)}, f32[3,1,3,384]{3,1,2,0:T(1,128)S(1)}, u32[]{:S(2)}, u32[]{:S(2)}) collective-permute-start(f32[3,1,3,384]{3,1,2,0:T(1,128)S(1)} %constant_dynamic-update-slice_fusion), channel_id=1, source_target_pairs={{0,1},{1,2},{2,3},{3,4},{4,5},{5,6},{6,7},{7,8},{8,9},{9,10},{10,1... | collective-permute-start | bytes 41480 | tf_op jit(solution)/shard_map/ppermute | solution.py:21
  99.6 10.6 %collective-permute-start.3 = (f32[3,1,16,384]{3,2,1,0:T(8,128)S(1)}, f32[3,1,16,384]{3,2,1,0:T(8,128)S(1)}, u32[]{:S(2)}, u32[]{:S(2)}) collective-permute-start(f32[3,1,16,384]{3,2,1,0:T(8,128)S(1)} %pad_maximum_fusion.1), channel_id=1, source_target_pairs={{1,0},{2,1},{3,2},{4,3},{5,4},{6,5},{7,6},{8,7},{9,8},{10,9},{11,1... | collective-permute-start | bytes 221192 | tf_op jit(solution)/shard_map/ppermute | solution.py:24
  108.2 3.3 collective-permute-start.2
  359.4 60.2 %copy-start.1 = (f32[2,16,4096]{2,1,0:T(8,128)S(1)}, f32[2,16,4096]{2,1,0:T(8,128)}, u32[]{:S(2)}) copy-start(f32[2,16,4096]{2,1,0:T(8,128)} %all-reduce.4.cloned.1.call-done) | copy-start | bytes 1572868
Sparse Core Ops, SparseCore 0:
  84.4 273.3 all-reduce.3
where the time goes:
time: 430 us
  matrix products  135 us (31%)
  waiting for transfers between devices  117 us (27%)
  blocking collectives  102 us (24%)
  starting transfers between devices  35 us (8%)
  between operations  16.9 us (4%)
  local copies, waits for them, and re-layouts  9.26 us (2%)
  other arithmetic  9.24 us (2%)
  loops' own time  5.16 us (1%)
    psum x1, waiting for transfers between devices, on_device(): factors = lax.psum(partial_value, ('gx', 'gy'))  111 us
    psum x1, blocking collectives, on_device(): e_pair = lax.psum(e_local, ('gx', 'gy'))  102 us
    ppermute x4, starting transfers between devices, with_halo(): lax.ppermute(lax.slice_in_dim(block, 0, width, axis=dim), axis, backward)  25.2 us
    dot_general x8, matrix products, forward(): jnp.dot(charges, sn, preferred_element_type=jnp.float32)  24.3 us
    dot_general x8, matrix products, forward(): jnp.dot(charges, cs, preferred_element_type=jnp.float32)  24.1 us
    dot_general x8, matrix products, backward(): lax.dot_general(charges, pblk, dims, preferred_element_type=jnp.float32)  23.4 us
    dot_general x8, matrix products, backward(): lax.dot_general(charges, qblk, dims, preferred_element_type=jnp.float32)  23 us
    dot_general x16, matrix products, trig(): lax.dot_general(glob, kvec, (((0,), (0,)), ((), ())), precision=lax.Preci...  18 us
  transfers between devices with their start and end apart: 9, of which 3 were waited for; matrix products, arithmetic and copies ran while one was open for 21% of the time, Pallas kernels for 0%

commit v1 on v0

v1 whole, which is shorter than its diff:
```python
import functools
import math

import jax
import jax.numpy as jnp
from jax import lax
from jax.experimental import pallas as pl
from jax.experimental.pallas import tpu as pltpu
from jax.sharding import PartitionSpec as P

WIDTH = 10.0
DEPTH = 12.0
CUT = 5.0
SMEAR = 1.5
SCALE = 0.25
NMAX = 8
TILE = 128
NBLK = 3
ATOMS = NBLK * TILE
QCH = 16
PCH = 16
KVEC = 4096
XS = 4
CORES = 2
TILES_C = 19
TILES_S = 18
ROWS = 8 * (TILES_C + TILES_S)
PAIRS = 8 * TILES_C
PADDED = 320
PART = PADDED // XS
MESH = pl.DeviceIdType.MESH
F32 = jnp.float32
BF16 = jnp.bfloat16
FAR = -1.0e30


def split(value):
    high = value.astype(BF16)
    return high, (value - high.astype(F32)).astype(BF16)


def unit_circle(turns):
    turns = turns - jnp.round(turns)
    half = turns * math.pi
    sq = half * half
    sine = 1.0 / 6227020800.0
    for term in (-1.0 / 39916800.0, 1.0 / 362880.0, -1.0 / 5040.0, 1.0 / 120.0, -1.0 / 6.0, 1.0):
        sine = sine * sq + term
    sine = sine * half
    cosine = 1.0 / 479001600.0
    for term in (-1.0 / 3628800.0, 1.0 / 40320.0, -1.0 / 720.0, 1.0 / 24.0, -0.5, 1.0):
        cosine = cosine * sq + term
    return 1.0 - 2.0 * sine * sine, 2.0 * sine * cosine


def dot3(a, b, dims):
    out = None
    for left, right in ((a[0], b[0]), (a[0], b[1]), (a[1], b[0])):
        term = lax.dot_general(left, right, (dims, ((), ())), preferred_element_type=F32)
        out = term if out is None else out + term
    return out


def kernel(
    sizes,
    pos_ref,
    feat_ref,
    nbr_ref,
    kidx_ref,
    wc_ref,
    wp_ref,
    energy_ref,
    force_ref,
    hood,
    mine,
    recv_c,
    acc_x,
    recv_x,
    sum_x,
    send_y,
    recv_y,
    recv_z,
    gath_y,
    full,
    vf,
    vh,
    vl,
    uf,
    uh,
    ul,
    zrow,
    lf,
    lh,
    ll,
    coef,
    codes,
    fi,
    zi,
    cmask,
    mbuf,
    pbuf,
    acc_p,
    fpair,
    halo_s,
    halo_r,
    rc_s,
    rc_r,
    rx_s,
    rx_r,
    ry_s,
    ry_r,
    rz_s,
    rz_r,
    gy_s,
    gy_r,
    gx_s,
    gx_r,
    gc_s,
    gc_r,
):
    cols_x, cols_y, ys, z_lo_n, z_hi_n = sizes
    zs = z_lo_n * z_hi_n
    sub = PART // ys
    gx = lax.axis_index("gx")
    gy = lax.axis_index("gy")
    z_lo, y = lax.div(gx, ys), lax.rem(gx, ys)
    z_hi = lax.div(gy, XS * CORES)
    x = lax.div(lax.rem(gy, XS * CORES), CORES)
    core = lax.rem(gy, CORES)
    z = z_hi * z_lo_n + z_lo
    other = 1 - core

    def core_dev():
        return (gx, gy + 1 - 2 * core)

    def x_dev(j):
        return (gx, (z_hi * XS + j) * CORES + core)

    def y_dev(j):
        return (z_lo * ys + j, gy)

    def z_dev(j):
        lo, hi = lax.rem(j, z_lo_n), lax.div(j, z_lo_n)
        return (lo * ys + y, (hi * XS + x) * CORES + core)

    def halo_dev(ix, iy):
        return (
            lax.rem(gx + (1 - ix) + cols_x, cols_x),
            lax.rem(gy + (1 - iy) + cols_y, cols_y),
        )

    halo = [(ix, iy) for ix in range(3) for iy in range(3) if (ix, iy) != (1, 1)]
    x_peers = [lax.rem(x + d, XS) for d in range(1, XS)]
    y_peers = [lax.rem(y + d, ys) for d in range(1, ys)]
    z_peers = [lax.rem(z + d, zs) for d in range(1, zs)]

    def copy(src, dst, send, recv, dev):
        return pltpu.make_async_remote_copy(
            src_ref=src, dst_ref=dst, send_sem=send, recv_sem=recv, device_id=dev, device_id_type=MESH
        )

    barrier = pltpu.get_barrier_semaphore()
    partners = [core_dev()]
    partners += [x_dev(j) for j in x_peers]
    partners += [y_dev(j) for j in y_peers]
    partners += [z_dev(j) for j in z_peers]
    partners += [halo_dev(ix, iy) for ix, iy in halo]
    for dev in partners:
        pl.semaphore_signal(barrier, inc=1, device_id=dev, device_id_type=MESH)

    feat = feat_ref[...]
    charges = jnp.dot(wc_ref[...], feat, preferred_element_type=F32).astype(BF16).astype(F32)
    pair_feat = jnp.dot(wp_ref[...], feat, preferred_element_type=F32)
    pos = pos_ref[...]
    hood[4, 0:PCH, :] = pair_feat
    hood[4, PCH:, :] = jnp.zeros((8, ATOMS), F32)
    hood[4, PCH : PCH + 3, :] = pos * (1.0 / CUT)

    order = lax.broadcasted_iota(jnp.int32, (8, ATOMS), 0).astype(F32) + 1.0
    gxf, gyf = gx.astype(F32), gy.astype(F32)
    cx, sx = unit_circle(order * ((pos[0:1] + gxf * WIDTH) * (1.0 / (cols_x * WIDTH))))
    cy, sy = unit_circle(order * ((pos[1:2] + gyf * WIDTH) * (1.0 / (cols_y * WIDTH))))
    cz, sz = unit_circle(order * (pos[2:3] * (1.0 / (NBLK * DEPTH))))

    def row(tile):
        return pl.ds(8 * tile, 8)

    for n in range(1, NMAX + 1):
        cyn, syn = cy[n - 1 : n], sy[n - 1 : n]
        cc, ss, sc, cs = cx * cyn, sx * syn, sx * cyn, cx * syn
        vf[row(8 + n), :] = cc - ss
        vf[row(8 - n), :] = cc + ss
        vf[row(TILES_C + 8 + n), :] = sc + cs
        vf[row(TILES_C + 8 - n), :] = sc - cs
    vf[row(8), :] = cx
    vf[row(TILES_C + 8), :] = sx
    vf[row(17), :] = cy
    vf[row(TILES_C + 17), :] = sy
    vf[row(18), :] = jnp.where(order < 1.5, 1.0, 0.0)
    vf[ROWS:, :] = jnp.zeros((PADDED - ROWS, ATOMS), F32)
    for c in range(QCH):
        uf[row(c), :] = cz * charges[c : c + 1]
        uf[row(QCH + c), :] = sz * charges[c : c + 1]
    high, low = split(vf[...])
    vh[...] = high
    vl[...] = low
    high, low = split(uf[...])
    uh[...] = high
    ul[...] = low

    pl.semaphore_wait(barrier, len(partners))

    core_copies = []
    for d in range(1, XS + 1):
        j = lax.rem(x + d, XS)
        rows = pl.ds(pl.multiple_of(j * PART, PART), PART)
        part = dot3(
            (vh[rows, :], vl[rows, :]), (uh[...], ul[...]), ((1,), (1,))
        )
        mine[0, j] = part[:, :TILE]
        mine[1, j] = part[:, TILE:]
        cp = copy(mine.at[other, j], recv_c.at[j], rc_s.at[j], rc_r.at[j], core_dev())
        cp.start()
        core_copies.append(cp)

    halo_copies = []
    for ix, iy in halo:
        k = 3 * ix + iy
        cp = copy(hood.at[4], hood.at[k], halo_s.at[k], halo_r.at[k], halo_dev(ix, iy))
        cp.start()
        halo_copies.append(cp)

    x_copies = []
    for d, cp in zip(range(1, XS + 1), core_copies):
        j = lax.rem(x + d, XS)
        cp.wait_recv()
        acc_x[j] = mine[core, j] + recv_c[j]
        if d < XS:
            xc = copy(acc_x.at[j], recv_x.at[x], rx_s.at[j], rx_r.at[x], x_dev(j))
            xc.start()
            x_copies.append(xc)

    fhigh, flow = split(pair_feat)
    fi[...] = jnp.concatenate([fhigh, flow, fhigh], axis=0)
    zrow[...] = jnp.zeros((8, ATOMS), F32)
    zown = pos[2:3] * (1.0 / CUT)
    lane = lax.broadcasted_iota(jnp.int32, (1, ATOMS), 1)
    wrap = NBLK * DEPTH / CUT
    for b in range(NBLK):
        shift = jnp.zeros((1, ATOMS), F32)
        if b + 2 < NBLK:
            shift = jnp.where(lane >= (b + 2) * TILE, -wrap, shift)
        if b >= 2:
            shift = jnp.where(lane < (b - 1) * TILE, wrap, shift)
        zi[b] = zown + shift
    tile_id = lax.broadcasted_iota(jnp.int32, (32, 32), 0)
    for b in range(NBLK):
        found = jnp.where(nbr_ref[b : b + 1, :] == tile_id, 1.0, FAR)
        found = jnp.max(found, axis=1, keepdims=True)
        cmask[:, b * TILE : (b + 1) * TILE] = jnp.broadcast_to(found, (32, TILE))
    acc_p[...] = jnp.zeros((4, 8, ATOMS), F32)
    for cp in halo_copies:
        cp.wait_recv()

    def pair_tile(t, carry):
        k = lax.div(t, NBLK)
        b = lax.rem(t, NBLK)
        cols = pl.ds(pl.multiple_of(b * TILE, TILE), TILE)
        block = hood[k, :, cols]
        high, low = split(block[:PCH])
        fj = jnp.concatenate([high, high, low], axis=0)
        mbuf[...] = lax.dot_general(fj, fi[...], (((0,), (0,)), ((), ())), preferred_element_type=F32)
        shift_x = (lax.div(k, 3) - 1).astype(F32) * (WIDTH / CUT)
        shift_y = (lax.rem(k, 3) - 1).astype(F32) * (WIDTH / CUT)
        which = lax.broadcasted_iota(jnp.int32, (8, TILE), 0)
        shift = jnp.where(which == 0, shift_x, jnp.where(which == 1, shift_y, 0.0))
        pbuf[...] = jnp.transpose(block[PCH:] + shift)
        xi = jnp.broadcast_to(hood[4, PCH : PCH + 1, :], (8, ATOMS))
        yi = jnp.broadcast_to(hood[4, PCH + 1 : PCH + 2, :], (8, ATOMS))
        zz = jnp.broadcast_to(zi[b], (8, ATOMS))
        limit = jnp.broadcast_to(cmask[pl.ds(t, 1), :], (8, ATOMS))
        ax, ay, az, ae = acc_p[0], acc_p[1], acc_p[2], acc_p[3]
        for g in range(TILE // 8):
            pj = pbuf[8 * g : 8 * g + 8, :]
            dx = xi - jnp.broadcast_to(pj[:, 0:1], (8, ATOMS))
            dy = yi - jnp.broadcast_to(pj[:, 1:2], (8, ATOMS))
            dz = zz - jnp.broadcast_to(pj[:, 2:3], (8, ATOMS))
            w = jnp.maximum(limit - (dx * dx + dy * dy + dz * dz), 0.0)
            mw = mbuf[8 * g : 8 * g + 8, :] * w
            ax = ax + mw * dx
            ay = ay + mw * dy
            az = az + mw * dz
            ae = ae + mw * w
        acc_p[0] = ax
        acc_p[1] = ay
        acc_p[2] = az
        acc_p[3] = ae
        return carry

    lax.fori_loop(0, 9 * NBLK, pair_tile, 0)
    force_scale = 4.0 * SCALE / CUT
    for i in range(3):
        fpair[i : i + 1, :] = force_scale * jnp.sum(acc_p[i], axis=0, keepdims=True)
    erow = jnp.sum(acc_p[3], axis=0, keepdims=True)
    own = jnp.sum(pair_feat * pair_feat, axis=0, keepdims=True)
    for b in range(NBLK):
        blk = slice(b * TILE, (b + 1) * TILE)
        named = jnp.maximum(cmask[4 * NBLK + b : 4 * NBLK + b + 1, blk], 0.0)
        fpair[3:4, blk] = erow[:, blk] - named * own[:, blk]
    epart = fpair[3:4, :TILE] + fpair[3:4, TILE : 2 * TILE] + fpair[3:4, 2 * TILE :]
    epart = epart * (0.5 * SCALE)

    for d, cp in enumerate(x_copies):
        j = x_peers[d]
        copy(acc_x.at[j], recv_x.at[j], rx_s.at[j], rx_r.at[j], x_dev(j)).wait_recv()
    recv_x[x] = acc_x[x]
    total = recv_x[0]
    for j in range(1, XS):
        total = total + recv_x[j]
    sum_x[...] = total
    for j in range(ys):
        send_y[j] = sum_x[sub * j : sub * (j + 1), :]
    y_copies = []
    for j in y_peers:
        cp = copy(send_y.at[j], recv_y.at[y], ry_s.at[j], ry_r.at[y], y_dev(j))
        cp.start()
        y_copies.append(cp)

    kx, ky, kz = kidx_ref[0:1, :], kidx_ref[1:2, :], kidx_ref[2:3, :]
    codes[0:1, :] = kx * 17 + ky
    codes[1:2, :] = kz
    coef[...] = jnp.zeros((2, PAIRS, TILE), F32)
    step = 512
    row_id = lax.broadcasted_iota(jnp.int32, (PAIRS, 1), 0)
    tile_of, sub_of = lax.div(row_id, 8), lax.rem(row_id, 8)
    nx = jnp.where(tile_of < 17, sub_of + 1, 0)
    ny = jnp.where(tile_of < 17, tile_of - 8, jnp.where(tile_of == 17, sub_of + 1, 0))
    none = 100000
    code = nx * 17 + ny
    plus = jnp.where((tile_of == 18) & (sub_of > 0), none, code)
    minus = jnp.where(tile_of == 18, none, -code)
    nz_of = lax.rem(lax.broadcasted_iota(jnp.int32, (TILE, 1), 0), 8) + 1

    def count(i, carry):
        cols = pl.ds(pl.multiple_of(i * step, step), step)
        xy, zc = codes[0:1, cols], codes[1:2, cols]
        on_z = jnp.where(zc == nz_of, 1.0, 0.0).astype(BF16)
        for s, target in ((0, plus), (1, minus)):
            on_xy = jnp.where(xy == target, 1.0, 0.0).astype(BF16)
            coef[s] += lax.dot_general(on_xy, on_z, (((1,), (1,)), ((), ())), preferred_element_type=F32)
        return carry

    lax.fori_loop(0, KVEC // step, count, 0)
    two_pi = 2.0 * math.pi
    wx = nx.astype(F32) * (two_pi / (cols_x * WIDTH))
    wy = ny.astype(F32) * (two_pi / (cols_y * WIDTH))
    wz = (lax.rem(lax.broadcasted_iota(jnp.int32, (1, TILE), 1), 8) + 1).astype(F32) * (two_pi / (NBLK * DEPTH))
    ksq = (wx * wx + wy * wy) + wz * wz
    norm = 1.0 / math.sqrt(cols_x * cols_y * ATOMS * KVEC)
    green = 4.0 * norm * jnp.exp(-0.5 * SMEAR * SMEAR * ksq) / ksq
    cplus, cminus = coef[0], coef[1]
    coef[0] = green * (cplus + cminus)
    coef[1] = green * (cplus - cminus)

    for j in y_peers:
        copy(send_y.at[j], recv_y.at[j], ry_s.at[j], ry_r.at[j], y_dev(j)).wait_recv()
    recv_y[y] = send_y[y]
    total = recv_y[0]
    for j in range(1, ys):
        total = total + recv_y[j]

    recv_z[z, 0:sub, :] = total
    recv_z[z, sub : sub + 1, :] = epart
    z_copies = []
    for j in z_peers:
        cp = copy(recv_z.at[z], recv_z.at[z], rz_s.at[j], rz_r.at[z], z_dev(j))
        cp.start()
        z_copies.append(cp)
    for j in z_peers:
        copy(recv_z.at[j], recv_z.at[j], rz_s.at[j], rz_r.at[j], z_dev(j)).wait_recv()
    total = recv_z[0]
    for j in range(1, zs):
        total = total + recv_z[j]
    gath_y[y] = total

    gy_copies = []
    for j in y_peers:
        cp = copy(gath_y.at[y], gath_y.at[y], gy_s.at[j], gy_r.at[y], y_dev(j))
        cp.start()
        gy_copies.append(cp)
    for j in y_peers:
        copy(gath_y.at[j], gath_y.at[j], gy_s.at[j], gy_r.at[j], y_dev(j)).wait_recv()
    esum = gath_y[0, sub : sub + 1, :]
    for j in range(1, ys):
        esum = esum + gath_y[j, sub : sub + 1, :]
    for j in range(ys):
        full[core, x, sub * j : sub * (j + 1), :] = gath_y[j, 0:sub, :]
    full[core, x, PART:, :] = jnp.broadcast_to(esum, (8, TILE))
    gx_copies = []
    for j in x_peers:
        cp = copy(full.at[core, x], full.at[core, x], gx_s.at[j], gx_r.at[x], x_dev(j))
        cp.start()
        gx_copies.append(cp)
    gc_copies = [copy(full.at[core, x], full.at[core, x], gc_s.at[x], gc_r.at[x], core_dev())]
    gc_copies[0].start()
    for j in x_peers:
        copy(full.at[core, j], full.at[core, j], gx_s.at[j], gx_r.at[j], x_dev(j)).wait_recv()
        cp = copy(full.at[core, j], full.at[core, j], gc_s.at[j], gc_r.at[j], core_dev())
        cp.start()
        gc_copies.append(cp)
    for j in range(XS):
        copy(full.at[other, j], full.at[other, j], gc_s.at[j], gc_r.at[j], core_dev()).wait_recv()

    def tile_of_full(half, t):
        return full[half, (8 * t) // PART, (8 * t) % PART : (8 * t) % PART + 8, :]

    sub_id = lax.broadcasted_iota(jnp.int32, (8, TILE), 0).astype(F32) + 1.0
    elong = jnp.zeros((8, TILE), F32)
    for t in range(TILES_C):
        a, b = coef[0, 8 * t : 8 * t + 8, :], coef[1, 8 * t : 8 * t + 8, :]
        cc, cs = tile_of_full(0, t), tile_of_full(1, t)
        if t < TILES_S:
            sc, ss = tile_of_full(0, TILES_C + t), tile_of_full(1, TILES_C + t)
            lcc, lss = a * cc - b * ss, a * ss - b * cc
            lsc, lcs = a * sc + b * cs, a * cs + b * sc
            elong = elong + ((lcc * cc + lss * ss) + (lsc * sc + lcs * cs))
        else:
            lcc, lcs = a * cc, a * cs
            elong = elong + (lcc * cc + lcs * cs)
        rc, rs = row(t), row(TILES_C + t)
        lf[rc, 0:128] = lcc
        lf[rc, 128:256] = lcs
        if t < TILES_S:
            lf[rs, 0:128] = lsc
            lf[rs, 128:256] = lss
            fx = sub_id if t < 17 else None
            fy = float(t - 8) if t < 17 else sub_id
            for base, factor in ((256, fx), (512, fy)):
                if factor is None:
                    lf[rc, base : base + 256] = jnp.zeros((8, 256), F32)
                    lf[rs, base : base + 256] = jnp.zeros((8, 256), F32)
                else:
                    lf[rc, base : base + 128] = factor * lsc
                    lf[rc, base + 128 : base + 256] = factor * lss
                    lf[rs, base : base + 128] = -(factor * lcc)
                    lf[rs, base + 128 : base + 256] = -(factor * lcs)
        else:
            lf[rc, 256:768] = jnp.zeros((8, 512), F32)
    lf[ROWS:, :] = jnp.zeros((PADDED - ROWS, 768), F32)
    high, low = split(lf[...])
    lh[...] = high
    ll[...] = low

    epair = full[0, 0, PART : PART + 1, :]
    for h, j in [(h, j) for h in range(CORES) for j in range(XS)][1:]:
        epair = epair + full[h, j, PART : PART + 1, :]
    etot = 0.5 * jnp.sum(elong, axis=0, keepdims=True) + epair
    energy_ref[0, 0] = jnp.sum(etot) * (1.0 / (cols_x * cols_y * ATOMS))

    vv = (vh[...], vl[...])
    grads = []
    for i in range(3):
        cols = slice(256 * i, 256 * i + 256)
        grads.append(dot3((lh[:, cols], ll[:, cols]), vv, ((0,), (0,))))
    u = uf[...]
    long_x = jnp.sum(u * grads[1], axis=0, keepdims=True)
    long_y = jnp.sum(u * grads[2], axis=0, keepdims=True)
    nz = (lax.rem(lax.broadcasted_iota(jnp.int32, (TILE, 1), 0), 8) + 1).astype(F32)
    curl = (u[:TILE] * grads[0][TILE:] - u[TILE:] * grads[0][:TILE]) * nz
    long_z = jnp.sum(curl, axis=0, keepdims=True)
    force_ref[0:1, :] = fpair[0:1, :] - (two_pi / (cols_x * WIDTH)) * long_x
    force_ref[1:2, :] = fpair[1:2, :] - (two_pi / (cols_y * WIDTH)) * long_y
    force_ref[2:3, :] = fpair[2:3, :] - (two_pi / (NBLK * DEPTH)) * long_z

    for group in (core_copies, halo_copies, x_copies, y_copies, z_copies, gy_copies, gx_copies, gc_copies):
        for cp in group:
            cp.wait_send()


def column(sizes, positions, features, nbr_tiles, kvec_index, weight_charge, weight_pair):
    cols_x, cols_y, ys, z_lo_n, z_hi_n = sizes
    zs = z_lo_n * z_hi_n
    sub = PART // ys
    vmem, dma = pltpu.VMEM, pltpu.SemaphoreType.DMA
    scratch = [
        vmem((9, PCH + 8, ATOMS), F32),
        vmem((CORES, XS, PART, TILE), F32),
        vmem((XS, PART, TILE), F32),
        vmem((XS, PART, TILE), F32),
        vmem((XS, PART, TILE), F32),
        vmem((PART, TILE), F32),
        vmem((ys, sub, TILE), F32),
        vmem((ys, sub, TILE), F32),
        vmem((zs, sub + 1, TILE), F32),
        vmem((ys, sub + 1, TILE), F32),
        vmem((CORES, XS, PART + 8, TILE), F32),
        vmem((PADDED, ATOMS), F32),
        vmem((PADDED, ATOMS), BF16),
        vmem((PADDED, ATOMS), BF16),
        vmem((2 * TILE, ATOMS), F32),
        vmem((2 * TILE, ATOMS), BF16),
        vmem((2 * TILE, ATOMS), BF16),
        vmem((8, ATOMS), F32),
        vmem((PADDED, 768), F32),
        vmem((PADDED, 768), BF16),
        vmem((PADDED, 768), BF16),
        vmem((2, PAIRS, TILE), F32),
        vmem((8, KVEC), jnp.int32),
        vmem((3 * PCH, ATOMS), BF16),
        vmem((NBLK, 1, ATOMS), F32),
        vmem((32, ATOMS), F32),
        vmem((TILE, ATOMS), F32),
        vmem((TILE, 8), F32),
        vmem((4, 8, ATOMS), F32),
        vmem((8, ATOMS), F32),
    ]
    for n in (9, XS, XS, ys, zs, ys, XS, XS):
        scratch += [dma((n,)), dma((n,))]
    whole = pl.BlockSpec(memory_space=pltpu.VMEM)
    energy, forces = pl.pallas_call(
        functools.partial(kernel, sizes),
        out_shape=(
            jax.ShapeDtypeStruct((1, 1), F32),
            jax.ShapeDtypeStruct((3, ATOMS), F32),
        ),
        in_specs=[whole] * 6,
        out_specs=(pl.BlockSpec(memory_space=pltpu.SMEM), whole),
        scratch_shapes=scratch,
        compiler_params=pltpu.CompilerParams(
            collective_id=0, has_side_effects=True, vmem_limit_bytes=40 * 1024 * 1024
        ),
    )(positions[0, 0], features[0, 0], nbr_tiles[0, 0], kvec_index, weight_charge, weight_pair)
    return energy[0, 0], forces[None, None]


def solution(mesh):
    cols_x, cols_y = mesh.shape["gx"], mesh.shape["gy"]
    z_lo_n = 2
    sizes = (cols_x, cols_y, cols_x // z_lo_n, z_lo_n, cols_y // (XS * CORES))
    cell = P("gx", "gy", None, None)
    return jax.shard_map(
        functools.partial(column, sizes),
        mesh=mesh,
        in_specs=(cell, cell, cell, P(), P(), P()),
        out_specs=(P(), cell),
        check_vma=False,
    )
```

time: 430 us -> 59 us (0.14)
  matrix products: 135 us -> 0 us
  waiting for transfers between devices: 117 us -> 0 us
  blocking collectives: 102 us -> 0 us
  Pallas kernels: 0 us -> 52.5 us
  starting transfers between devices: 35 us -> 0 us
  between operations: 16.9 us -> 2.48 us
  other arithmetic: 9.24 us -> 0 us
  local copies, waits for them, and re-layouts: 9.26 us -> 3.72 us
  loops' own time: 5.16 us -> 0 us
    dot_general x61 -> x0, matrix products: 135 us -> none  [the longest x8 24.3 us: forward(): jnp.dot(charges, sn, preferred_element_type=jnp.float32)]
    psum x1 -> x0, waiting for transfers between devices: 111 us -> none  [on_device(): factors = lax.psum(partial_value, ('gx', 'gy'))]
    psum x1 -> x0, blocking collectives: 102 us -> none  [on_device(): e_pair = lax.psum(e_local, ('gx', 'gy'))]
    pallas_call x0 -> x1, Pallas kernels: none -> 52.5 us  [column(): pl.pallas_call(functools.partial(kernel, sizes), out_shape=(jax.ShapeDtyp...]
    ppermute x8 -> x0, starting transfers between devices: 35 us -> none  [the longest x4 25.2 us: with_halo(): lax.ppermute(lax.slice_in_dim(block, 0, width, axis=dim), axis, backward)]
    ppermute x8 -> x0, waiting for transfers between devices: 6.58 us -> none  [the longest x4 6.57 us: with_halo(): lax.ppermute(lax.slice_in_dim(block, block.shape[dim] - width, None, axis...]
    sub x4 -> x0, other arithmetic: 5.38 us -> none  [the longest x3 5.37 us: block_terms(): delta = own_pos[None, :, :, None] - picked_pos[:, :, None, :]]
    another operation x3 -> x0, loops' own time: 5.16 us -> none  [the longest x1 4.49 us: pair_terms(): lax.map(one_block, (jnp.arange(nblk), own_pos, own_feat, rows))]
  transfers between devices with their start and end apart: 9 -> 0, of which waited for: 3 -> 0; matrix products, arithmetic and copies ran while one was open for 21% -> 0% of each run, Pallas kernels for 0% -> 0%
where the time goes in v1:
time: 59 us; the launch traced here: 58.7 us
  Pallas kernels  52.5 us (89%)
  local copies, waits for them, and re-layouts  3.72 us (6%)
  between operations  2.48 us (4%)
    pallas_call x1, Pallas kernels, column(): pl.pallas_call(functools.partial(kernel, sizes), out_shape=(jax.ShapeDtyp...  52.5 us
    unnamed x15, local copies, waits for them, and re-layouts  3.72 us

profile of v1, /device:TPU:1, one launch (start us, length us, event | category | flops | bytes accessed | tf_op | source)
XLA Modules:
  0.0 58.7 jit_solution(657140778942208125)
XLA Ops:
  0.6 0.0 copy-start.5
  0.6 0.0 copy-start.4
  0.6 0.7 %copy-done.5 = s32[1,1,3,32]{3,1,2,0:T(1,128)S(1)} copy-done((s32[1,1,3,32]{3,1,2,0:T(1,128)S(1)}, s32[1,1,3,32]{3,1,2,0:T(1,128)}, u32[]{:S(2)}) %copy-start.5) | copy-done | bytes 408
  1.3 0.0 copy-done.4
  1.3 0.0 copy-start.2
  1.3 0.0 copy-start.3
  1.3 0.7 %copy-done.2 = bf16[16,128]{1,0:T(8,128)(2,1)S(1)} copy-done((bf16[16,128]{1,0:T(8,128)(2,1)S(1)}, bf16[16,128]{1,0:T(8,128)(2,1)}, u32[]{:S(2)}) %copy-start.2) | copy-done | bytes 4120
  2.0 0.0 copy-done.3
  2.0 0.0 copy-start
  2.0 0.9 %copy-done = bf16[1,1,128,384]{3,2,1,0:T(8,128)(2,1)S(1)} copy-done((bf16[1,1,128,384]{3,2,1,0:T(8,128)(2,1)S(1)}, bf16[1,1,128,384]{3,2,1,0:T(8,128)(2,1)}, u32[]{:S(2)}) %copy-start) | copy-done | bytes 98328
  2.9 0.0 copy-start.1
  2.9 0.8 %copy-done.1 = s32[3,4096]{1,0:T(4,128)S(1)} copy-done((s32[3,4096]{1,0:T(4,128)S(1)}, s32[3,4096]{1,0:T(4,128)}, u32[]{:S(2)}) %copy-start.1) | copy-done | bytes 49176
  3.8 52.5 %shard_map.77 = (f32[1,1]{1,0:T(1,128)}, f32[3,384]{1,0:T(4,128)S(1)}) custom-call(f32[3,384]{1,0:T(4,128)S(1)} %bitcast.10, bf16[128,384]{1,0:T(8,128)(2,1)S(1)} %bitcast.9, s32[3,32]{1,0:T(4,128)S(1)} %bitcast.11, s32[3,4096]{1,0:T(4,128)S(1)} %copy-done.1, bf16[16,128]{1,0:T(8,128)(2,1)S(1)} %copy-done.2, bf16[16,128]{1,0:T(8,128)(2,1)S(1)} %copy-done.3), custom_call_target="tpu_custom_call" | custom-call | tf_op jit(solution)/shard_map/pallas_call | solution.py:520
  56.3 0.6 %copy.8 = f32[1,1,3,384]{3,1,2,0:T(1,128)} copy(f32[1,1,3,384]{3,2,1,0:T(4,128)S(1)} %bitcast.12) | data formatting | bytes 9216
  (2 shorter events, 0.0 us)
Async XLA Ops:
  0.6 0.7 %copy-start.5 = (s32[1,1,3,32]{3,1,2,0:T(1,128)S(1)}, s32[1,1,3,32]{3,1,2,0:T(1,128)}, u32[]{:S(2)}) copy-start(s32[1,1,3,32]{3,1,2,0:T(1,128)} %param.8) | copy-start | bytes 1156
  0.6 0.7 %copy-start.4 = (f32[1,1,3,384]{3,1,2,0:T(1,128)S(1)}, f32[1,1,3,384]{3,1,2,0:T(1,128)}, u32[]{:S(2)}) copy-start(f32[1,1,3,384]{3,1,2,0:T(1,128)} %param.6) | copy-start | bytes 13828
  1.3 0.7 %copy-start.2 = (bf16[16,128]{1,0:T(8,128)(2,1)S(1)}, bf16[16,128]{1,0:T(8,128)(2,1)}, u32[]{:S(2)}) copy-start(bf16[16,128]{1,0:T(8,128)(2,1)} %wc_ref.1) | copy-start | bytes 12292
  1.3 0.7 %copy-start.3 = (bf16[16,128]{1,0:T(8,128)(2,1)S(1)}, bf16[16,128]{1,0:T(8,128)(2,1)}, u32[]{:S(2)}) copy-start(bf16[16,128]{1,0:T(8,128)(2,1)} %wp_ref.1) | copy-start | bytes 12292
  2.0 0.9 %copy-start = (bf16[1,1,128,384]{3,2,1,0:T(8,128)(2,1)S(1)}, bf16[1,1,128,384]{3,2,1,0:T(8,128)(2,1)}, u32[]{:S(2)}) copy-start(bf16[1,1,128,384]{3,2,1,0:T(8,128)(2,1)} %param.7) | copy-start | bytes 294916
  2.9 0.8 %copy-start.1 = (s32[3,4096]{1,0:T(4,128)S(1)}, s32[3,4096]{1,0:T(4,128)}, u32[]{:S(2)}) copy-start(s32[3,4096]{1,0:T(4,128)} %kidx_ref.1) | copy-start | bytes 147460

commit v2 on v1

v2 whole, which is shorter than its diff:
```python
import functools
import math

import jax
import jax.numpy as jnp
from jax import lax
from jax.experimental import pallas as pl
from jax.experimental.pallas import tpu as pltpu
from jax.sharding import PartitionSpec as P

WIDTH = 10.0
DEPTH = 12.0
CUT = 5.0
SMEAR = 1.5
SCALE = 0.25
NMAX = 8
TILE = 128
NBLK = 3
ATOMS = NBLK * TILE
QCH = 16
PCH = 16
KVEC = 4096
XS = 4
CORES = 2
TILES_C = 19
TILES_S = 18
ROWS = 8 * (TILES_C + TILES_S)
PAIRS = 8 * TILES_C
PADDED = 320
PART = PADDED // XS
MESH = pl.DeviceIdType.MESH
F32 = jnp.float32
BF16 = jnp.bfloat16
FAR = -1.0e30


def split(value):
    high = value.astype(BF16)
    return high, (value - high.astype(F32)).astype(BF16)


def unit_circle(turns):
    turns = turns - jnp.round(turns)
    half = turns * math.pi
    sq = half * half
    sine = 1.0 / 6227020800.0
    for term in (-1.0 / 39916800.0, 1.0 / 362880.0, -1.0 / 5040.0, 1.0 / 120.0, -1.0 / 6.0, 1.0):
        sine = sine * sq + term
    sine = sine * half
    cosine = 1.0 / 479001600.0
    for term in (-1.0 / 3628800.0, 1.0 / 40320.0, -1.0 / 720.0, 1.0 / 24.0, -0.5, 1.0):
        cosine = cosine * sq + term
    return 1.0 - 2.0 * sine * sine, 2.0 * sine * cosine


def dot3(a, b, dims):
    out = None
    for left, right in ((a[0], b[0]), (a[0], b[1]), (a[1], b[0])):
        term = lax.dot_general(left, right, (dims, ((), ())), preferred_element_type=F32)
        out = term if out is None else out + term
    return out


def kernel(
    sizes,
    pos_hbm,
    feat_hbm,
    nbr_hbm,
    kidx_hbm,
    wc_hbm,
    wp_hbm,
    energy_ref,
    force_ref,
    pos_ref,
    feat_ref,
    nbr_ref,
    kidx_ref,
    wc_ref,
    wp_ref,
    hood,
    mine,
    recv_c,
    acc_x,
    send_p,
    recv_p,
    recv_z,
    gath_p,
    full,
    e_z,
    e_p,
    e_c,
    vf,
    vh,
    vl,
    uf,
    uh,
    ul,
    lf,
    lh,
    ll,
    coef,
    codes,
    fi,
    pi,
    cmask,
    mbuf,
    acc_p,
    acc_e,
    fpair,
    in_s,
    halo_s,
    halo_r,
    rc_s,
    rc_r,
    rp_s,
    rp_r,
    rz_s,
    rz_r,
    gp_s,
    gp_r,
    gc_s,
    gc_r,
    ez_s,
    ez_r,
    ep_s,
    ep_r,
    ec_s,
    ec_r,
):
    cols_x, cols_y, ys, z_lo_n, z_hi_n = sizes
    zs = z_lo_n * z_hi_n
    sub = PART // ys
    gx = lax.axis_index("gx")
    gy = lax.axis_index("gy")
    z_lo, y = lax.div(gx, ys), lax.rem(gx, ys)
    z_hi = lax.div(gy, XS * CORES)
    x = lax.div(lax.rem(gy, XS * CORES), CORES)
    core = lax.rem(gy, CORES)
    z = z_hi * z_lo_n + z_lo
    other = 1 - core
    me = x * ys + y

    inputs = []
    pairs = ((feat_hbm, feat_ref), (wp_hbm, wp_ref), (pos_hbm, pos_ref), (wc_hbm, wc_ref), (nbr_hbm, nbr_ref), (kidx_hbm, kidx_ref))
    for i, (src, dst) in enumerate(pairs):
        cp = pltpu.make_async_copy(src, dst, in_s.at[i])
        cp.start()
        inputs.append(cp)

    core_dev = (gx, gy + 1 - 2 * core)

    def plane_dev(j, k):
        return (z_lo * ys + k, (z_hi * XS + j) * CORES + core)

    def z_dev(j):
        lo, hi = lax.rem(j, z_lo_n), lax.div(j, z_lo_n)
        return (lo * ys + y, (hi * XS + x) * CORES + core)

    def halo_dev(ix, iy):
        return (
            lax.rem(gx + (1 - ix) + cols_x, cols_x),
            lax.rem(gy + (1 - iy) + cols_y, cols_y),
        )

    def around(value, step, size):
        return lax.rem(value + step, size) if step else value

    halo = [(ix, iy) for ix in range(3) for iy in range(3) if (ix, iy) != (1, 1)]
    x_order = [around(x, d, XS) for d in range(XS)]
    y_order = [around(y, d, ys) for d in range(ys)]
    plane = [(j, k) for n, j in enumerate(x_order) for m, k in enumerate(y_order) if n or m]
    z_peers = [around(z, d, zs) for d in range(1, zs)]

    def copy(src, dst, send, recv, dev):
        return pltpu.make_async_remote_copy(
            src_ref=src, dst_ref=dst, send_sem=send, recv_sem=recv, device_id=dev, device_id_type=MESH
        )

    barrier = pltpu.get_barrier_semaphore()
    partners = [core_dev]
    partners += [plane_dev(j, k) for j, k in plane]
    partners += [z_dev(j) for j in z_peers]
    partners += [halo_dev(ix, iy) for ix, iy in halo]
    for dev in partners:
        pl.semaphore_signal(barrier, inc=1, device_id=dev, device_id_type=MESH)

    def landed(ref, sem):
        copy(ref, ref, sem, sem, core_dev).wait_recv()

    def left(ref, sem):
        copy(ref, ref, sem, sem, core_dev).wait_send()


    for cp in inputs[:3]:
        cp.wait()
    feat = feat_ref[...]
    pair_feat = jnp.dot(wp_ref[...], feat, preferred_element_type=F32)
    hood[4, 0:PCH, :] = pair_feat
    hood[4, PCH:, :] = jnp.zeros((8, ATOMS), F32)
    for i in range(3):
        hood[4, PCH + i : PCH + i + 1, :] = pos_ref[i] * (1.0 / CUT)
    pl.semaphore_wait(barrier, len(partners))
    for ix, iy in halo:
        k = 3 * ix + iy
        copy(hood.at[4], hood.at[k], halo_s, halo_r, halo_dev(ix, iy)).start()

    inputs[3].wait()
    charges = jnp.dot(wc_ref[...], feat, preferred_element_type=F32).astype(BF16).astype(F32)
    order = lax.broadcasted_iota(jnp.int32, (8, ATOMS), 0).astype(F32) + 1.0
    gxf, gyf = gx.astype(F32), gy.astype(F32)
    cx, sx = unit_circle(order * ((pos_ref[0] + gxf * WIDTH) * (1.0 / (cols_x * WIDTH))))
    cy, sy = unit_circle(order * ((pos_ref[1] + gyf * WIDTH) * (1.0 / (cols_y * WIDTH))))
    cz, sz = unit_circle(order * (pos_ref[2] * (1.0 / (NBLK * DEPTH))))

    def row(tile):
        return pl.ds(8 * tile, 8)

    for n in range(1, NMAX + 1):
        cyn, syn = cy[n - 1 : n], sy[n - 1 : n]
        cc, ss, sc, cs = cx * cyn, sx * syn, sx * cyn, cx * syn
        vf[row(8 + n), :] = cc - ss
        vf[row(8 - n), :] = cc + ss
        vf[row(TILES_C + 8 + n), :] = sc + cs
        vf[row(TILES_C + 8 - n), :] = sc - cs
    vf[row(8), :] = cx
    vf[row(TILES_C + 8), :] = sx
    vf[row(17), :] = cy
    vf[row(TILES_C + 17), :] = sy
    vf[row(18), :] = jnp.where(order < 1.5, 1.0, 0.0)
    vf[ROWS:, :] = jnp.zeros((PADDED - ROWS, ATOMS), F32)
    for c in range(QCH):
        uf[row(c), :] = cz * charges[c : c + 1]
        uf[row(QCH + c), :] = sz * charges[c : c + 1]
    high, low = split(vf[...])
    vh[...] = high
    vl[...] = low
    high, low = split(uf[...])
    uh[...] = high
    ul[...] = low

    rotated = x_order[1:] + x_order[:1]
    for j in rotated:
        rows = pl.ds(pl.multiple_of(j * PART, PART), PART)
        part = dot3((vh[rows, :], vl[rows, :]), (uh[...], ul[...]), ((1,), (1,)))
        mine[0, j] = part[:, :TILE]
        mine[1, j] = part[:, TILE:]
        copy(mine.at[other, j], recv_c.at[j], rc_s, rc_r.at[j], core_dev).start()

    for j in rotated:
        landed(recv_c.at[j], rc_r.at[j])
        acc_x[...] = mine[core, j] + recv_c[j]
        for k in range(ys):
            send_p[j, k] = acc_x[sub * k : sub * (k + 1), :]
        for m, k in enumerate(y_order):
            if j is x and m == 0:
                recv_p[me] = send_p[x, y]
            else:
                copy(send_p.at[j, k], recv_p.at[me], rp_s, rp_r, plane_dev(j, k)).start()

    fhigh, flow = split(pair_feat)
    stacked = jnp.concatenate([fhigh, flow, fhigh], axis=0).astype(F32)
    fi[...] = jnp.transpose(stacked).astype(BF16)
    own_pos = jnp.transpose(hood[4, PCH:, :])
    for i in range(3):
        pi[i] = jnp.broadcast_to(own_pos[:, i : i + 1], (ATOMS, TILE))
    inputs[4].wait()
    tile_id = lax.broadcasted_iota(jnp.int32, (32, 32), 0)
    for b in range(NBLK):
        found = jnp.where(nbr_ref[b] == tile_id, 1.0, FAR)
        found = jnp.max(found, axis=1, keepdims=True)
        cmask[:, b * TILE : (b + 1) * TILE] = jnp.broadcast_to(found, (32, TILE))
    acc_p[...] = jnp.zeros((3, ATOMS, TILE), F32)
    acc_e[...] = jnp.zeros((32, TILE), F32)
    wrap = NBLK * DEPTH / CUT

    def couple(k, slot):
        high, low = split(hood[k, 0:PCH, :])
        fj = jnp.concatenate([high, high, low], axis=0)
        mbuf[slot] = jnp.dot(fi[...], fj, preferred_element_type=F32)

    def pair_column(k, slot):
        shift_x = (lax.div(k, 3) - 1).astype(F32) * (WIDTH / CUT)
        shift_y = (lax.rem(k, 3) - 1).astype(F32) * (WIDTH / CUT)
        xj = hood[k, PCH : PCH + 1, :] + shift_x
        yj = hood[k, PCH + 1 : PCH + 2, :] + shift_y
        zj = hood[k, PCH + 2 : PCH + 3, :]
        limits = [cmask[pl.ds(NBLK * k + c, 1), :] for c in range(NBLK)]
        ae = acc_e[...]
        for b in range(NBLK):
            for g in range(TILE // 32):
                rows = slice(b * TILE + 32 * g, b * TILE + 32 * g + 32)
                xi, yi, zi = pi[0, rows, :], pi[1, rows, :], pi[2, rows, :]
                ax, ay, az = acc_p[0, rows, :], acc_p[1, rows, :], acc_p[2, rows, :]
                for c in range(NBLK):
                    cols = slice(c * TILE, (c + 1) * TILE)
                    zc = zj[:, cols]
                    if c - b == 2:
                        zc = zc - wrap
                    if b - c == 2:
                        zc = zc + wrap
                    limit = limits[c][:, b * TILE : (b + 1) * TILE]
                    dx, dy, dz = xi - xj[:, cols], yi - yj[:, cols], zi - zc
                    w = jnp.maximum(limit - (dx * dx + dy * dy + dz * dz), 0.0)
                    mw = mbuf[slot, rows, cols] * w
                    ax = ax + mw * dx
                    ay = ay + mw * dy
                    az = az + mw * dz
                    ae = ae + mw * w
                acc_p[0, rows, :] = ax
                acc_p[1, rows, :] = ay
                acc_p[2, rows, :] = az
        acc_e[...] = ae

    couple(4, 0)
    pair_column(jnp.int32(4), 0)

    inputs[5].wait()
    kx, ky, kz = kidx_ref[0:1, :], kidx_ref[1:2, :], kidx_ref[2:3, :]
    codes[0:1, :] = kx * 17 + ky
    codes[1:2, :] = kz
    coef[...] = jnp.zeros((2, PAIRS, TILE), F32)
    step = 512
    row_id = lax.broadcasted_iota(jnp.int32, (PAIRS, 1), 0)
    tile_of, sub_of = lax.div(row_id, 8), lax.rem(row_id, 8)
    nx = jnp.where(tile_of < 17, sub_of + 1, 0)
    ny = jnp.where(tile_of < 17, tile_of - 8, jnp.where(tile_of == 17, sub_of + 1, 0))
    none = 100000
    code = nx * 17 + ny
    plus = jnp.where((tile_of == 18) & (sub_of > 0), none, code)
    minus = jnp.where(tile_of == 18, none, -code)
    nz_of = lax.rem(lax.broadcasted_iota(jnp.int32, (TILE, 1), 0), 8) + 1

    def count(i, carry):
        cols = pl.ds(pl.multiple_of(i * step, step), step)
        xy, zc = codes[0:1, cols], codes[1:2, cols]
        on_z = jnp.where(zc == nz_of, 1.0, 0.0).astype(BF16)
        for s, target in ((0, plus), (1, minus)):
            on_xy = jnp.where(xy == target, 1.0, 0.0).astype(BF16)
            coef[s] += lax.dot_general(on_xy, on_z, (((1,), (1,)), ((), ())), preferred_element_type=F32)
        return carry

    lax.fori_loop(0, KVEC // step, count, 0)
    two_pi = 2.0 * math.pi
    wx = nx.astype(F32) * (two_pi / (cols_x * WIDTH))
    wy = ny.astype(F32) * (two_pi / (cols_y * WIDTH))
    wz = (lax.rem(lax.broadcasted_iota(jnp.int32, (1, TILE), 1), 8) + 1).astype(F32) * (two_pi / (NBLK * DEPTH))
    ksq = (wx * wx + wy * wy) + wz * wz
    norm = 1.0 / math.sqrt(cols_x * cols_y * ATOMS * KVEC)
    green = 4.0 * norm * jnp.exp(-0.5 * SMEAR * SMEAR * ksq) / ksq
    cplus, cminus = coef[0], coef[1]
    coef[0] = green * (cplus + cminus)
    coef[1] = green * (cplus - cminus)

    landed(recv_p.at[1:], rp_r)
    total = recv_p[0]
    for s in range(1, XS * ys):
        total = total + recv_p[s]

    recv_z[z] = total
    for j in z_peers:
        copy(recv_z.at[z], recv_z.at[z], rz_s, rz_r, z_dev(j)).start()

    landed(hood.at[0:8], halo_r)
    couple(5, 1)

    def pair_step(i, carry):
        slot = lax.rem(i, 2)
        couple(lax.rem(i + 5, 9), 1 - slot)
        pair_column(lax.rem(i + 4, 9), slot)
        return carry

    lax.fori_loop(1, 8, pair_step, 0)
    pair_column(jnp.int32(3), 0)
    own = jnp.sum(pair_feat * pair_feat, axis=0, keepdims=True)
    epart = jnp.sum(acc_e[...], axis=0, keepdims=True)
    for b in range(NBLK):
        blk = slice(b * TILE, (b + 1) * TILE)
        named = jnp.maximum(cmask[4 * NBLK + b : 4 * NBLK + b + 1, blk], 0.0)
        epart = epart - named * own[:, blk]
    e_z[z] = epart * (0.5 * SCALE)
    for j in z_peers:
        copy(e_z.at[z], e_z.at[z], ez_s, ez_r, z_dev(j)).start()
    force_scale = 4.0 * SCALE / CUT
    ones = jnp.ones((8, TILE), BF16)
    for i in range(3):
        high, low = split(acc_p[i])
        sums = lax.dot_general(ones, high, (((1,), (1,)), ((), ())), preferred_element_type=F32)
        sums = sums + lax.dot_general(ones, low, (((1,), (1,)), ((), ())), preferred_element_type=F32)
        fpair[i : i + 1, :] = force_scale * sums[0:1]

    landed(recv_z.at[1:], rz_r)
    total = recv_z[0]
    for j in range(1, zs):
        total = total + recv_z[j]

    gath_p[me] = total
    for j, k in plane:
        copy(gath_p.at[me], gath_p.at[me], gp_s, gp_r.at[x], plane_dev(j, k)).start()
    landed(e_z.at[1:], ez_r)
    esum = e_z[0]
    for j in range(1, zs):
        esum = esum + e_z[j]
    e_p[me] = esum
    for j, k in plane:
        copy(e_p.at[me], e_p.at[me], ep_s, ep_r, plane_dev(j, k)).start()
    for j in x_order:
        landed(gath_p.at[pl.ds(j * ys, ys - 1 if j is x else ys)], gp_r.at[j])
        for k in range(ys):
            full[core, j, sub * k : sub * (k + 1), :] = gath_p[j * ys + k]
        copy(full.at[core, j], full.at[core, j], gc_s, gc_r, core_dev).start()
    landed(full.at[other], gc_r)

    def tile_of_full(half, t):
        return full[half, (8 * t) // PART, (8 * t) % PART : (8 * t) % PART + 8, :]

    sub_id = lax.broadcasted_iota(jnp.int32, (8, TILE), 0).astype(F32) + 1.0
    elong = jnp.zeros((8, TILE), F32)
    for t in range(TILES_C):
        a, b = coef[0, 8 * t : 8 * t + 8, :], coef[1, 8 * t : 8 * t + 8, :]
        cc, cs = tile_of_full(0, t), tile_of_full(1, t)
        if t < TILES_S:
            sc, ss = tile_of_full(0, TILES_C + t), tile_of_full(1, TILES_C + t)
            lcc, lss = a * cc - b * ss, a * ss - b * cc
            lsc, lcs = a * sc + b * cs, a * cs + b * sc
            elong = elong + ((lcc * cc + lss * ss) + (lsc * sc + lcs * cs))
        else:
            lcc, lcs = a * cc, a * cs
            elong = elong + (lcc * cc + lcs * cs)
        rc, rs = row(t), row(TILES_C + t)
        lf[rc, 0:128] = lcc
        lf[rc, 128:256] = lcs
        if t < TILES_S:
            lf[rs, 0:128] = lsc
            lf[rs, 128:256] = lss
            fx = sub_id if t < 17 else None
            fy = float(t - 8) if t < 17 else sub_id
            for base, factor in ((256, fx), (512, fy)):
                if factor is None:
                    lf[rc, base : base + 256] = jnp.zeros((8, 256), F32)
                    lf[rs, base : base + 256] = jnp.zeros((8, 256), F32)
                else:
                    lf[rc, base : base + 128] = factor * lsc
                    lf[rc, base + 128 : base + 256] = factor * lss
                    lf[rs, base : base + 128] = -(factor * lcc)
                    lf[rs, base + 128 : base + 256] = -(factor * lcs)
        else:
            lf[rc, 256:768] = jnp.zeros((8, 512), F32)
    lf[ROWS:, :] = jnp.zeros((PADDED - ROWS, 768), F32)
    high, low = split(lf[...])
    lh[...] = high
    ll[...] = low

    vv = (vh[...], vl[...])
    grads = []
    for i in range(3):
        cols = slice(256 * i, 256 * i + 256)
        grads.append(dot3((lh[:, cols], ll[:, cols]), vv, ((0,), (0,))))
    u = uf[...]
    long_x = jnp.sum(u * grads[1], axis=0, keepdims=True)
    long_y = jnp.sum(u * grads[2], axis=0, keepdims=True)
    nz = (lax.rem(lax.broadcasted_iota(jnp.int32, (TILE, 1), 0), 8) + 1).astype(F32)
    curl = (u[:TILE] * grads[0][TILE:] - u[TILE:] * grads[0][:TILE]) * nz
    long_z = jnp.sum(curl, axis=0, keepdims=True)
    force_ref[0] = fpair[0:1, :] - (two_pi / (cols_x * WIDTH)) * long_x
    force_ref[1] = fpair[1:2, :] - (two_pi / (cols_y * WIDTH)) * long_y
    force_ref[2] = fpair[2:3, :] - (two_pi / (NBLK * DEPTH)) * long_z

    landed(e_p.at[1:], ep_r)
    esum = e_p[0]
    for s in range(1, XS * ys):
        esum = esum + e_p[s]
    e_c[core] = esum
    copy(e_c.at[core], e_c.at[core], ec_s, ec_r, core_dev).start()
    landed(e_c.at[other], ec_r)
    etot = 0.5 * jnp.sum(elong, axis=0, keepdims=True) + (e_c[0] + e_c[1])
    energy_ref[0, 0] = jnp.sum(etot) * (1.0 / (cols_x * cols_y * ATOMS))
    left(hood.at[0:8], halo_s)
    left(mine.at[0], rc_s)
    left(recv_p.at[1:], rp_s)
    left(recv_z.at[1:], rz_s)
    left(gath_p.at[1:], gp_s)
    left(full.at[core], gc_s)
    left(e_z.at[1:], ez_s)
    left(e_p.at[1:], ep_s)
    left(e_c.at[core], ec_s)


def column(sizes, positions, features, nbr_tiles, kvec_index, weight_charge, weight_pair):
    cols_x, cols_y, ys, z_lo_n, z_hi_n = sizes
    zs = z_lo_n * z_hi_n
    ps = XS * ys
    sub = PART // ys
    vmem, dma = pltpu.VMEM, pltpu.SemaphoreType.DMA
    scratch = [
        vmem((3, 1, ATOMS), F32),
        vmem((128, ATOMS), BF16),
        vmem((NBLK, 1, 32), jnp.int32),
        vmem((3, KVEC), jnp.int32),
        vmem((QCH, 128), BF16),
        vmem((PCH, 128), BF16),
        vmem((9, PCH + 8, ATOMS), F32),
        vmem((CORES, XS, PART, TILE), F32),
        vmem((XS, PART, TILE), F32),
        vmem((PART, TILE), F32),
        vmem((XS, ys, sub, TILE), F32),
        vmem((ps, sub, TILE), F32),
        vmem((zs, sub, TILE), F32),
        vmem((ps, sub, TILE), F32),
        vmem((CORES, XS, PART, TILE), F32),
        vmem((zs, 1, TILE), F32),
        vmem((ps, 1, TILE), F32),
        vmem((CORES, 1, TILE), F32),
        vmem((PADDED, ATOMS), F32),
        vmem((PADDED, ATOMS), BF16),
        vmem((PADDED, ATOMS), BF16),
        vmem((2 * TILE, ATOMS), F32),
        vmem((2 * TILE, ATOMS), BF16),
        vmem((2 * TILE, ATOMS), BF16),
        vmem((PADDED, 768), F32),
        vmem((PADDED, 768), BF16),
        vmem((PADDED, 768), BF16),
        vmem((2, PAIRS, TILE), F32),
        vmem((8, KVEC), jnp.int32),
        vmem((ATOMS, 3 * PCH), BF16),
        vmem((3, ATOMS, TILE), F32),
        vmem((32, ATOMS), F32),
        vmem((2, ATOMS, ATOMS), F32),
        vmem((3, ATOMS, TILE), F32),
        vmem((32, TILE), F32),
        vmem((8, ATOMS), F32),
        dma((6,)),
    ]
    one, each_x = dma(()), dma((XS,))
    scratch += [one, one, one, each_x, one, one, one, one, one, each_x, one, one, one, one, one, one, one, one]
    anywhere = pl.BlockSpec(memory_space=pl.ANY)
    energy, forces = pl.pallas_call(
        functools.partial(kernel, sizes),
        out_shape=(
            jax.ShapeDtypeStruct((1, 1), F32),
            jax.ShapeDtypeStruct((3, 1, ATOMS), F32),
        ),
        in_specs=[anywhere] * 6,
        out_specs=(pl.BlockSpec(memory_space=pltpu.SMEM), pl.BlockSpec(memory_space=pltpu.VMEM)),
        scratch_shapes=scratch,
        compiler_params=pltpu.CompilerParams(
            collective_id=0, has_side_effects=True, vmem_limit_bytes=60 * 1024 * 1024
        ),
    )(
        positions.reshape(3, 1, ATOMS),
        features[0, 0],
        nbr_tiles.reshape(NBLK, 1, 32),
        kvec_index,
        weight_charge,
        weight_pair,
    )
    return energy[0, 0], forces.reshape(1, 1, 3, ATOMS)


def solution(mesh):
    cols_x, cols_y = mesh.shape["gx"], mesh.shape["gy"]
    z_lo_n = 2
    sizes = (cols_x, cols_y, cols_x // z_lo_n, z_lo_n, cols_y // (XS * CORES))
    cell = P("gx", "gy", None, None)
    return jax.shard_map(
        functools.partial(column, sizes),
        mesh=mesh,
        in_specs=(cell, cell, cell, P(), P(), P()),
        out_specs=(P(), cell),
        check_vma=False,
    )
```

time: 59 us -> 45.9 us (0.78)
  Pallas kernels: 52.5 us -> 42.6 us
  local copies, waits for them, and re-layouts: 3.72 us -> 0.63 us
    pallas_call x1, Pallas kernels: 52.5 us -> 42.6 us  [column(): pl.pallas_call(functools.partial(kernel, sizes), out_shape=(jax.ShapeDtyp...]
    unnamed x15 -> x3, local copies, waits for them, and re-layouts: 3.72 us -> 0.63 us
where the time goes in v2:
time: 45.9 us; the launch traced here: 45.7 us
  Pallas kernels  42.6 us (93%)
  between operations  2.42 us (5%)
  local copies, waits for them, and re-layouts  0.63 us (1%)
    pallas_call x1, Pallas kernels, column(): pl.pallas_call(functools.partial(kernel, sizes), out_shape=(jax.ShapeDtyp...  42.6 us

profile of v2, /device:TPU:1, one launch (start us, length us, event | category | flops | bytes accessed | tf_op | source)
XLA Modules:
  0.0 45.7 jit_solution(15813975930237903274)
XLA Ops:
  0.6 42.6 %shard_map.77 = (f32[1,1]{1,0:T(1,128)}, f32[3,1,384]{2,1,0:T(1,128)}) custom-call(f32[3,1,384]{2,1,0:T(1,128)} %bitcast.8, bf16[128,384]{1,0:T(8,128)(2,1)} %bitcast.7, s32[3,1,32]{2,1,0:T(1,128)} %bitcast.10, s32[3,4096]{1,0:T(4,128)} %kidx_hbm.1, bf16[16,128]{1,0:T(8,128)(2,1)} %wc_hbm.1, bf16[16,128]{1,0:T(8,128)(2,1)} %wp_hbm.1), custom_call_target="tpu_custom_call" | custom-call | tf_op jit(solution)/shard_map/pallas_call | solution.py:536
  43.2 0.0 copy-start
  43.9 0.0 copy-done
  43.9 0.6 %copy.12 = f32[1,1,3,384]{3,1,2,0:T(1,128)} copy(f32[1,1,3,384]{3,1,2,0:T(1,128)S(1)} %bitcast.9) | data formatting | bytes 9216
Async XLA Ops:
  43.2 0.7 %copy-start = (f32[3,1,384]{2,1,0:T(1,128)S(1)}, f32[3,1,384]{2,1,0:T(1,128)}, u32[]{:S(2)}) copy-start(f32[3,1,384]{2,1,0:T(1,128)} %get-tuple-element.5) | copy-start | bytes 13828

commit v3 on v2

--- a/solution.py
+++ b/solution.py
@@ -169,6 +169,8 @@
     x_order = [around(x, d, XS) for d in range(XS)]
     y_order = [around(y, d, ys) for d in range(ys)]
     plane = [(j, k) for n, j in enumerate(x_order) for m, k in enumerate(y_order) if n or m]
+    hops = lambda jk: min(jk[0], XS - jk[0]) + min(jk[1], ys - jk[1])
+    outward = sorted([(j, k) for j in range(XS) for k in range(ys)], key=hops)
     z_peers = [around(z, d, zs) for d in range(1, zs)]
 
     def copy(src, dst, send, recv, dev):
@@ -199,11 +201,6 @@
     hood[4, PCH:, :] = jnp.zeros((8, ATOMS), F32)
     for i in range(3):
         hood[4, PCH + i : PCH + i + 1, :] = pos_ref[i] * (1.0 / CUT)
-    pl.semaphore_wait(barrier, len(partners))
-    for ix, iy in halo:
-        k = 3 * ix + iy
-        copy(hood.at[4], hood.at[k], halo_s, halo_r, halo_dev(ix, iy)).start()
-
     inputs[3].wait()
     charges = jnp.dot(wc_ref[...], feat, preferred_element_type=F32).astype(BF16).astype(F32)
     order = lax.broadcasted_iota(jnp.int32, (8, ATOMS), 0).astype(F32) + 1.0
@@ -238,21 +235,29 @@
     uh[...] = high
     ul[...] = low
 
-    rotated = x_order[1:] + x_order[:1]
+    rotated = [x_order[i] for i in (2, 1, 3, 0)]
+    far = [y_order[i] for i in sorted(range(ys), key=lambda i: -min(i, ys - i))]
     for j in rotated:
         rows = pl.ds(pl.multiple_of(j * PART, PART), PART)
-        part = dot3((vh[rows, :], vl[rows, :]), (uh[...], ul[...]), ((1,), (1,)))
+        part = lax.dot_general(vh[rows, :], uh[...], (((1,), (1,)), ((), ())), preferred_element_type=F32)
         mine[0, j] = part[:, :TILE]
         mine[1, j] = part[:, TILE:]
+
+    pl.semaphore_wait(barrier, len(partners))
+    for j in rotated:
         copy(mine.at[other, j], recv_c.at[j], rc_s, rc_r.at[j], core_dev).start()
+    for ix, iy in halo:
+        k = 3 * ix + iy
+        copy(hood.at[4], hood.at[k], halo_s, halo_r, halo_dev(ix, iy)).start()
+
 
     for j in rotated:
         landed(recv_c.at[j], rc_r.at[j])
         acc_x[...] = mine[core, j] + recv_c[j]
         for k in range(ys):
             send_p[j, k] = acc_x[sub * k : sub * (k + 1), :]
-        for m, k in enumerate(y_order):
-            if j is x and m == 0:
+        for k in far:
+            if j is x and k is y:
                 recv_p[me] = send_p[x, y]
             else:
                 copy(send_p.at[j, k], recv_p.at[me], rp_s, rp_r, plane_dev(j, k)).start()
@@ -351,15 +356,6 @@
     coef[0] = green * (cplus + cminus)
     coef[1] = green * (cplus - cminus)
 
-    landed(recv_p.at[1:], rp_r)
-    total = recv_p[0]
-    for s in range(1, XS * ys):
-        total = total + recv_p[s]
-
-    recv_z[z] = total
-    for j in z_peers:
-        copy(recv_z.at[z], recv_z.at[z], rz_s, rz_r, z_dev(j)).start()
-
     landed(hood.at[0:8], halo_r)
     couple(5, 1)
 
@@ -369,7 +365,22 @@
         pair_column(lax.rem(i + 4, 9), slot)
         return carry
 
-    lax.fori_loop(1, 8, pair_step, 0)
+    lax.fori_loop(1, 4, pair_step, 0)
+
+    landed(recv_p.at[1:], rp_r)
+    total = recv_p[0]
+    for s in range(1, XS * ys):
+        total = total + recv_p[s]
+
+    recv_z[z] = total
+    for j in sorted(range(zs), key=lambda j: min(j, zs - j)):
+
+        @pl.when(j != z)
+        def _(j=j):
+            copy(recv_z.at[z], recv_z.at[z], rz_s, rz_r, z_dev(j)).start()
+
+
+    lax.fori_loop(4, 8, pair_step, 0)
     pair_column(jnp.int32(3), 0)
     own = jnp.sum(pair_feat * pair_feat, axis=0, keepdims=True)
     epart = jnp.sum(acc_e[...], axis=0, keepdims=True)
@@ -377,9 +388,8 @@
         blk = slice(b * TILE, (b + 1) * TILE)
         named = jnp.maximum(cmask[4 * NBLK + b : 4 * NBLK + b + 1, blk], 0.0)
         epart = epart - named * own[:, blk]
-    e_z[z] = epart * (0.5 * SCALE)
-    for j in z_peers:
-        copy(e_z.at[z], e_z.at[z], ez_s, ez_r, z_dev(j)).start()
+    e_c[core] = epart * (0.5 * SCALE)
+    copy(e_c.at[core], e_c.at[core], ec_s, ec_r, core_dev).start()
     force_scale = 4.0 * SCALE / CUT
     ones = jnp.ones((8, TILE), BF16)
     for i in range(3):
@@ -388,14 +398,23 @@
         sums = sums + lax.dot_general(ones, low, (((1,), (1,)), ((), ())), preferred_element_type=F32)
         fpair[i : i + 1, :] = force_scale * sums[0:1]
 
+    landed(e_c.at[other], ec_r)
+    e_z[z] = e_c[0] + e_c[1]
+    for j in z_peers:
+        copy(e_z.at[z], e_z.at[z], ez_s, ez_r, z_dev(j)).start()
+
     landed(recv_z.at[1:], rz_r)
     total = recv_z[0]
     for j in range(1, zs):
         total = total + recv_z[j]
 
     gath_p[me] = total
-    for j, k in plane:
-        copy(gath_p.at[me], gath_p.at[me], gp_s, gp_r.at[x], plane_dev(j, k)).start()
+    for j, k in outward:
+
+        @pl.when(j * ys + k != me)
+        def _(j=j, k=k):
+            copy(gath_p.at[me], gath_p.at[me], gp_s, gp_r.at[x], plane_dev(j, k)).start()
+
     landed(e_z.at[1:], ez_r)
     esum = e_z[0]
     for j in range(1, zs):
@@ -446,15 +465,13 @@
         else:
             lf[rc, 256:768] = jnp.zeros((8, 512), F32)
     lf[ROWS:, :] = jnp.zeros((PADDED - ROWS, 768), F32)
-    high, low = split(lf[...])
-    lh[...] = high
-    ll[...] = low
+    lh[...] = lf[...].astype(BF16)
 
     vv = (vh[...], vl[...])
     grads = []
     for i in range(3):
         cols = slice(256 * i, 256 * i + 256)
-        grads.append(dot3((lh[:, cols], ll[:, cols]), vv, ((0,), (0,))))
+        grads.append(lax.dot_general(lh[:, cols], vv[0], (((0,), (0,)), ((), ())), preferred_element_type=F32))
     u = uf[...]
     long_x = jnp.sum(u * grads[1], axis=0, keepdims=True)
     long_y = jnp.sum(u * grads[2], axis=0, keepdims=True)
@@ -469,10 +486,7 @@
     esum = e_p[0]
     for s in range(1, XS * ys):
         esum = esum + e_p[s]
-    e_c[core] = esum
-    copy(e_c.at[core], e_c.at[core], ec_s, ec_r, core_dev).start()
-    landed(e_c.at[other], ec_r)
-    etot = 0.5 * jnp.sum(elong, axis=0, keepdims=True) + (e_c[0] + e_c[1])
+    etot = 0.5 * jnp.sum(elong, axis=0, keepdims=True) + esum
     energy_ref[0, 0] = jnp.sum(etot) * (1.0 / (cols_x * cols_y * ATOMS))
     left(hood.at[0:8], halo_s)
     left(mine.at[0], rc_s)
@@ -537,7 +551,7 @@
         functools.partial(kernel, sizes),
         out_shape=(
             jax.ShapeDtypeStruct((1, 1), F32),
-            jax.ShapeDtypeStruct((3, 1, ATOMS), F32),
+            pltpu.VMEM((3, 1, ATOMS), F32),
         ),
         in_specs=[anywhere] * 6,
         out_specs=(pl.BlockSpec(memory_space=pltpu.SMEM), pl.BlockSpec(memory_space=pltpu.VMEM)),

time: 45.9 us -> 42.9 us (0.935)
  Pallas kernels: 42.6 us -> 39.8 us
    pallas_call x1, Pallas kernels: 42.6 us -> 39.8 us  [column(): pl.pallas_call(functools.partial(kernel, sizes), out_shape=(jax.ShapeDtyp...]
where the time goes in v3:
time: 42.9 us; the launch traced here: 42.7 us
  Pallas kernels  39.8 us (93%)
  between operations  2.33 us (5%)
  local copies, waits for them, and re-layouts  0.6 us (1%)
    pallas_call x1, Pallas kernels, column(): pl.pallas_call(functools.partial(kernel, sizes), out_shape=(jax.ShapeDtyp...  39.8 us

profile of v3, /device:TPU:1, one launch (start us, length us, event | category | flops | bytes accessed | tf_op | source)
XLA Modules:
  0.0 42.7 jit_solution(8670242227235089788)
XLA Ops:
  0.6 39.8 %shard_map.77 = (f32[1,1]{1,0:T(1,128)}, f32[3,1,384]{2,1,0:T(1,128)S(1)}) custom-call(f32[3,1,384]{2,1,0:T(1,128)} %bitcast.9, bf16[128,384]{1,0:T(8,128)(2,1)} %bitcast.8, s32[3,1,32]{2,1,0:T(1,128)} %bitcast.10, s32[3,4096]{1,0:T(4,128)} %kidx_hbm.1, bf16[16,128]{1,0:T(8,128)(2,1)} %wc_hbm.1, bf16[16,128]{1,0:T(8,128)(2,1)} %wp_hbm.1), custom_call_target="tpu_custom_call" | custom-call | tf_op jit(solution)/shard_map/pallas_call | solution.py:550
  40.4 0.6 %copy.11 = f32[1,1,3,384]{3,1,2,0:T(1,128)} copy(f32[1,1,3,384]{3,1,2,0:T(1,128)S(1)} %bitcast.7) | data formatting | bytes 9216

commit v4 on v3

--- a/solution.py
+++ b/solution.py
@@ -53,14 +53,6 @@
     return 1.0 - 2.0 * sine * sine, 2.0 * sine * cosine
 
 
-def dot3(a, b, dims):
-    out = None
-    for left, right in ((a[0], b[0]), (a[0], b[1]), (a[1], b[0])):
-        term = lax.dot_general(left, right, (dims, ((), ())), preferred_element_type=F32)
-        out = term if out is None else out + term
-    return out
-
-
 def kernel(
     sizes,
     pos_hbm,
@@ -69,8 +61,7 @@
     kidx_hbm,
     wc_hbm,
     wp_hbm,
-    energy_ref,
-    force_ref,
+    out_ref,
     pos_ref,
     feat_ref,
     nbr_ref,
@@ -88,16 +79,11 @@
     full,
     e_z,
     e_p,
-    e_c,
     vf,
     vh,
-    vl,
     uf,
     uh,
-    ul,
     lf,
-    lh,
-    ll,
     coef,
     codes,
     fi,
@@ -109,7 +95,9 @@
     fpair,
     in_s,
     halo_s,
-    halo_r,
+    halo_x,
+    halo_y,
+    halo_d,
     rc_s,
     rc_r,
     rp_s,
@@ -124,8 +112,6 @@
     ez_r,
     ep_s,
     ep_r,
-    ec_s,
-    ec_r,
 ):
     cols_x, cols_y, ys, z_lo_n, z_hi_n = sizes
     zs = z_lo_n * z_hi_n
@@ -152,7 +138,7 @@
     def plane_dev(j, k):
         return (z_lo * ys + k, (z_hi * XS + j) * CORES + core)
 
-    def z_dev(j):
+    def z_dev(j, core=core):
         lo, hi = lax.rem(j, z_lo_n), lax.div(j, z_lo_n)
         return (lo * ys + y, (hi * XS + x) * CORES + core)
 
@@ -165,7 +151,7 @@
     def around(value, step, size):
         return lax.rem(value + step, size) if step else value
 
-    halo = [(ix, iy) for ix in range(3) for iy in range(3) if (ix, iy) != (1, 1)]
+    halo = [(0, 1), (2, 1), (1, 0), (1, 2)]
     x_order = [around(x, d, XS) for d in range(XS)]
     y_order = [around(y, d, ys) for d in range(ys)]
     plane = [(j, k) for n, j in enumerate(x_order) for m, k in enumerate(y_order) if n or m]
@@ -179,9 +165,12 @@
         )
 
     barrier = pltpu.get_barrier_semaphore()
-    partners = [core_dev]
-    partners += [plane_dev(j, k) for j, k in plane]
-    partners += [z_dev(j) for j in z_peers]
+    steps = [(n, m) for n in range(XS) for m in range(ys) if n or m]
+    steps = sorted(steps, key=lambda nm: -(min(nm[0], XS - nm[0]) + min(nm[1], ys - nm[1])))
+    partners = [plane_dev(x_order[n], y_order[m]) for n, m in steps]
+    partners += [z_dev(z_peers[d - 1]) for d in sorted(range(1, zs), key=lambda d: -min(d, zs - d))]
+    partners += [z_dev(j, other) for j in z_peers]
+    partners += [core_dev]
     partners += [halo_dev(ix, iy) for ix, iy in halo]
     for dev in partners:
         pl.semaphore_signal(barrier, inc=1, device_id=dev, device_id_type=MESH)
@@ -198,7 +187,6 @@
     feat = feat_ref[...]
     pair_feat = jnp.dot(wp_ref[...], feat, preferred_element_type=F32)
     hood[4, 0:PCH, :] = pair_feat
-    hood[4, PCH:, :] = jnp.zeros((8, ATOMS), F32)
     for i in range(3):
         hood[4, PCH + i : PCH + i + 1, :] = pos_ref[i] * (1.0 / CUT)
     inputs[3].wait()
@@ -226,14 +214,11 @@
     vf[row(18), :] = jnp.where(order < 1.5, 1.0, 0.0)
     vf[ROWS:, :] = jnp.zeros((PADDED - ROWS, ATOMS), F32)
     for c in range(QCH):
-        uf[row(c), :] = cz * charges[c : c + 1]
-        uf[row(QCH + c), :] = sz * charges[c : c + 1]
-    high, low = split(vf[...])
-    vh[...] = high
-    vl[...] = low
-    high, low = split(uf[...])
-    uh[...] = high
-    ul[...] = low
+        h, first = c // 8, 8 * (c % 8)
+        uf[h, first : first + 8, :] = cz * charges[c : c + 1]
+        uf[h, 64 + first : 72 + first, :] = sz * charges[c : c + 1]
+    vh[...] = vf[...].astype(BF16)
+    uh[...] = uf[...].reshape(2 * TILE, ATOMS).astype(BF16)
 
     rotated = [x_order[i] for i in (2, 1, 3, 0)]
     far = [y_order[i] for i in sorted(range(ys), key=lambda i: -min(i, ys - i))]
@@ -248,7 +233,7 @@
         copy(mine.at[other, j], recv_c.at[j], rc_s, rc_r.at[j], core_dev).start()
     for ix, iy in halo:
         k = 3 * ix + iy
-        copy(hood.at[4], hood.at[k], halo_s, halo_r, halo_dev(ix, iy)).start()
+        copy(hood.at[4], hood.at[k], halo_s, halo_x if iy == 1 else halo_y, halo_dev(ix, iy)).start()
 
 
     for j in rotated:
@@ -265,7 +250,8 @@
     fhigh, flow = split(pair_feat)
     stacked = jnp.concatenate([fhigh, flow, fhigh], axis=0).astype(F32)
     fi[...] = jnp.transpose(stacked).astype(BF16)
-    own_pos = jnp.transpose(hood[4, PCH:, :])
+    own_pos = [pos_ref[i] * (1.0 / CUT) for i in range(3)] + [jnp.zeros((5, ATOMS), F32)]
+    own_pos = jnp.transpose(jnp.concatenate(own_pos, axis=0))
     for i in range(3):
         pi[i] = jnp.broadcast_to(own_pos[:, i : i + 1], (ATOMS, TILE))
     inputs[4].wait()
@@ -319,6 +305,80 @@
     couple(4, 0)
     pair_column(jnp.int32(4), 0)
 
+    landed(hood.at[0:2], halo_x)
+    for ix in (0, 2):
+        for iy in (0, 2):
+            copy(hood.at[3 * ix + 1], hood.at[3 * ix + iy], halo_s, halo_d, halo_dev(1, iy)).start()
+    landed(hood.at[0:2], halo_y)
+
+    def pair_columns(column_of):
+        couple(column_of(0), 0)
+
+        def pair_step(i, carry):
+            slot = lax.rem(i, 2)
+            couple(column_of(i + 1), 1 - slot)
+            pair_column(column_of(i), slot)
+            return carry
+
+        lax.fori_loop(0, 3, pair_step, 0)
+        pair_column(jnp.int32(column_of(3)), 1)
+
+    pair_columns(lambda i: 2 * i + 1)
+
+    landed(recv_p.at[1:], rp_r)
+    total = recv_p[0]
+    for s in range(1, XS * ys):
+        total = total + recv_p[s]
+
+    recv_z[z] = total
+    for j in sorted(range(zs), key=lambda j: min(j, zs - j)):
+
+        @pl.when(j != z)
+        def _(j=j):
+            copy(recv_z.at[z], recv_z.at[z], rz_s, rz_r, z_dev(j)).start()
+
+
+    landed(hood.at[0:4], halo_d)
+    pair_columns(lambda i: 2 * i + 2 * (i // 2) if isinstance(i, int) else 2 * i + 2 * lax.div(i, 2))
+    own = jnp.sum(pair_feat * pair_feat, axis=0, keepdims=True)
+    epart = jnp.sum(acc_e[...], axis=0, keepdims=True)
+    for b in range(NBLK):
+        blk = slice(b * TILE, (b + 1) * TILE)
+        named = jnp.maximum(cmask[4 * NBLK + b : 4 * NBLK + b + 1, blk], 0.0)
+        epart = epart - named * own[:, blk]
+    part = z * CORES + core
+    e_z[part] = epart * (0.5 * SCALE)
+    for j in z_peers:
+        copy(e_z.at[part], e_z.at[part], ez_s, ez_r, z_dev(j)).start()
+        copy(e_z.at[part], e_z.at[part], ez_s, ez_r, z_dev(j, other)).start()
+    copy(e_z.at[part], e_z.at[part], ez_s, ez_r, core_dev).start()
+    force_scale = 4.0 * SCALE / CUT
+    ones = jnp.ones((8, TILE), BF16)
+    for i in range(3):
+        high, low = split(acc_p[i])
+        sums = lax.dot_general(ones, high, (((1,), (1,)), ((), ())), preferred_element_type=F32)
+        sums = sums + lax.dot_general(ones, low, (((1,), (1,)), ((), ())), preferred_element_type=F32)
+        fpair[i : i + 1, :] = force_scale * sums[0:1]
+
+    landed(recv_z.at[1:], rz_r)
+    total = recv_z[0]
+    for j in range(1, zs):
+        total = total + recv_z[j]
+
+    gath_p[me] = total
+    for j, k in outward:
+
+        @pl.when(j * ys + k != me)
+        def _(j=j, k=k):
+            copy(gath_p.at[me], gath_p.at[me], gp_s, gp_r.at[x], plane_dev(j, k)).start()
+
+    landed(e_z.at[1:], ez_r)
+    esum = e_z[0]
+    for j in range(1, CORES * zs):
+        esum = esum + e_z[j]
+    e_p[me] = esum
+    for j, k in plane:
+        copy(e_p.at[me], e_p.at[me], ep_s, ep_r, plane_dev(j, k)).start()
     inputs[5].wait()
     kx, ky, kz = kidx_ref[0:1, :], kidx_ref[1:2, :], kidx_ref[2:3, :]
     codes[0:1, :] = kx * 17 + ky
@@ -354,140 +414,65 @@
     green = 4.0 * norm * jnp.exp(-0.5 * SMEAR * SMEAR * ksq) / ksq
     cplus, cminus = coef[0], coef[1]
     coef[0] = green * (cplus + cminus)
-    coef[1] = green * (cplus - cminus)
-
-    landed(hood.at[0:8], halo_r)
-    couple(5, 1)
-
-    def pair_step(i, carry):
-        slot = lax.rem(i, 2)
-        couple(lax.rem(i + 5, 9), 1 - slot)
-        pair_column(lax.rem(i + 4, 9), slot)
-        return carry
-
-    lax.fori_loop(1, 4, pair_step, 0)
-
-    landed(recv_p.at[1:], rp_r)
-    total = recv_p[0]
-    for s in range(1, XS * ys):
-        total = total + recv_p[s]
-
-    recv_z[z] = total
-    for j in sorted(range(zs), key=lambda j: min(j, zs - j)):
-
-        @pl.when(j != z)
-        def _(j=j):
-            copy(recv_z.at[z], recv_z.at[z], rz_s, rz_r, z_dev(j)).start()
-
-
-    lax.fori_loop(4, 8, pair_step, 0)
-    pair_column(jnp.int32(3), 0)
-    own = jnp.sum(pair_feat * pair_feat, axis=0, keepdims=True)
-    epart = jnp.sum(acc_e[...], axis=0, keepdims=True)
-    for b in range(NBLK):
-        blk = slice(b * TILE, (b + 1) * TILE)
-        named = jnp.maximum(cmask[4 * NBLK + b : 4 * NBLK + b + 1, blk], 0.0)
-        epart = epart - named * own[:, blk]
-    e_c[core] = epart * (0.5 * SCALE)
-    copy(e_c.at[core], e_c.at[core], ec_s, ec_r, core_dev).start()
-    force_scale = 4.0 * SCALE / CUT
-    ones = jnp.ones((8, TILE), BF16)
-    for i in range(3):
-        high, low = split(acc_p[i])
-        sums = lax.dot_general(ones, high, (((1,), (1,)), ((), ())), preferred_element_type=F32)
-        sums = sums + lax.dot_general(ones, low, (((1,), (1,)), ((), ())), preferred_element_type=F32)
-        fpair[i : i + 1, :] = force_scale * sums[0:1]
-
-    landed(e_c.at[other], ec_r)
-    e_z[z] = e_c[0] + e_c[1]
-    for j in z_peers:
-        copy(e_z.at[z], e_z.at[z], ez_s, ez_r, z_dev(j)).start()
-
-    landed(recv_z.at[1:], rz_r)
-    total = recv_z[0]
-    for j in range(1, zs):
-        total = total + recv_z[j]
-
-    gath_p[me] = total
-    for j, k in outward:
-
-        @pl.when(j * ys + k != me)
-        def _(j=j, k=k):
-            copy(gath_p.at[me], gath_p.at[me], gp_s, gp_r.at[x], plane_dev(j, k)).start()
-
-    landed(e_z.at[1:], ez_r)
-    esum = e_z[0]
-    for j in range(1, zs):
-        esum = esum + e_z[j]
-    e_p[me] = esum
-    for j, k in plane:
-        copy(e_p.at[me], e_p.at[me], ep_s, ep_r, plane_dev(j, k)).start()
+    lanes = lax.broadcasted_iota(jnp.int32, (1, TILE), 1)
+    coef[1] = jnp.where(lanes < 64, -green, green) * (cplus - cminus)
+
     for j in x_order:
         landed(gath_p.at[pl.ds(j * ys, ys - 1 if j is x else ys)], gp_r.at[j])
         for k in range(ys):
             full[core, j, sub * k : sub * (k + 1), :] = gath_p[j * ys + k]
         copy(full.at[core, j], full.at[core, j], gc_s, gc_r, core_dev).start()
+    sub_id = lax.broadcasted_iota(jnp.int32, (8, TILE), 0).astype(F32) + 1.0
+    nz = (lax.rem(lax.broadcasted_iota(jnp.int32, (64, 1), 0), 8) + 1).astype(F32)
+
+    def field(h):
+        def tile_of(t):
+            return full[h, (8 * t) // PART, (8 * t) % PART : (8 * t) % PART + 8, :]
+
+        elong = jnp.zeros((8, TILE), F32)
+        for t in range(TILES_C):
+            a, b = coef[0, 8 * t : 8 * t + 8, :], coef[1, 8 * t : 8 * t + 8, :]
+            rc, rs = row(t), row(TILES_C + t)
+            xc = tile_of(t)
+            if t == TILES_S:
+                lc = a * xc
+                elong = elong + lc * xc
+                lf[rc, 0:TILE] = lc
+                lf[rc, TILE:] = jnp.zeros((8, 2 * TILE), F32)
+                continue
+            xs = tile_of(TILES_C + t)
+            lc = a * xc + b * pltpu.roll(xs, 64, 1)
+            ls = a * xs - b * pltpu.roll(xc, 64, 1)
+            elong = elong + (lc * xc + ls * xs)
+            lf[rc, 0:TILE] = lc
+            lf[rs, 0:TILE] = ls
+            fx = sub_id if t < 17 else 0.0
+            fy = float(t - 8) if t < 17 else sub_id
+            for base, factor in ((TILE, fx), (2 * TILE, fy)):
+                lf[rc, base : base + TILE] = factor * ls
+                lf[rs, base : base + TILE] = -(factor * lc)
+        lf[ROWS:, :] = jnp.zeros((PADDED - ROWS, 3 * TILE), F32)
+        grad = lax.dot_general(lf[...].astype(BF16), vh[...], (((0,), (0,)), ((), ())), preferred_element_type=F32)
+        u = uf[h]
+        gx_ = jnp.sum(u * grad[TILE : 2 * TILE], axis=0, keepdims=True)
+        gy_ = jnp.sum(u * grad[2 * TILE :], axis=0, keepdims=True)
+        curl = (u[:64] * grad[64:TILE] - u[64:] * grad[:64]) * nz
+        return elong, gx_, gy_, jnp.sum(curl, axis=0, keepdims=True)
+
+    mine_half = field(core)
     landed(full.at[other], gc_r)
-
-    def tile_of_full(half, t):
-        return full[half, (8 * t) // PART, (8 * t) % PART : (8 * t) % PART + 8, :]
-
-    sub_id = lax.broadcasted_iota(jnp.int32, (8, TILE), 0).astype(F32) + 1.0
-    elong = jnp.zeros((8, TILE), F32)
-    for t in range(TILES_C):
-        a, b = coef[0, 8 * t : 8 * t + 8, :], coef[1, 8 * t : 8 * t + 8, :]
-        cc, cs = tile_of_full(0, t), tile_of_full(1, t)
-        if t < TILES_S:
-            sc, ss = tile_of_full(0, TILES_C + t), tile_of_full(1, TILES_C + t)
-            lcc, lss = a * cc - b * ss, a * ss - b * cc
-            lsc, lcs = a * sc + b * cs, a * cs + b * sc
-            elong = elong + ((lcc * cc + lss * ss) + (lsc * sc + lcs * cs))
-        else:
-            lcc, lcs = a * cc, a * cs
-            elong = elong + (lcc * cc + lcs * cs)
-        rc, rs = row(t), row(TILES_C + t)
-        lf[rc, 0:128] = lcc
-        lf[rc, 128:256] = lcs
-        if t < TILES_S:
-            lf[rs, 0:128] = lsc
-            lf[rs, 128:256] = lss
-            fx = sub_id if t < 17 else None
-            fy = float(t - 8) if t < 17 else sub_id
-            for base, factor in ((256, fx), (512, fy)):
-                if factor is None:
-                    lf[rc, base : base + 256] = jnp.zeros((8, 256), F32)
-                    lf[rs, base : base + 256] = jnp.zeros((8, 256), F32)
-                else:
-                    lf[rc, base : base + 128] = factor * lsc
-                    lf[rc, base + 128 : base + 256] = factor * lss
-                    lf[rs, base : base + 128] = -(factor * lcc)
-                    lf[rs, base + 128 : base + 256] = -(factor * lcs)
-        else:
-            lf[rc, 256:768] = jnp.zeros((8, 512), F32)
-    lf[ROWS:, :] = jnp.zeros((PADDED - ROWS, 768), F32)
-    lh[...] = lf[...].astype(BF16)
-
-    vv = (vh[...], vl[...])
-    grads = []
-    for i in range(3):
-        cols = slice(256 * i, 256 * i + 256)
-        grads.append(lax.dot_general(lh[:, cols], vv[0], (((0,), (0,)), ((), ())), preferred_element_type=F32))
-    u = uf[...]
-    long_x = jnp.sum(u * grads[1], axis=0, keepdims=True)
-    long_y = jnp.sum(u * grads[2], axis=0, keepdims=True)
-    nz = (lax.rem(lax.broadcasted_iota(jnp.int32, (TILE, 1), 0), 8) + 1).astype(F32)
-    curl = (u[:TILE] * grads[0][TILE:] - u[TILE:] * grads[0][:TILE]) * nz
-    long_z = jnp.sum(curl, axis=0, keepdims=True)
-    force_ref[0] = fpair[0:1, :] - (two_pi / (cols_x * WIDTH)) * long_x
-    force_ref[1] = fpair[1:2, :] - (two_pi / (cols_y * WIDTH)) * long_y
-    force_ref[2] = fpair[2:3, :] - (two_pi / (NBLK * DEPTH)) * long_z
+    elong, long_x, long_y, long_z = (p + q for p, q in zip(mine_half, field(other)))
+    out_ref[0] = fpair[0:1, :] - (two_pi / (cols_x * WIDTH)) * long_x
+    out_ref[1] = fpair[1:2, :] - (two_pi / (cols_y * WIDTH)) * long_y
+    out_ref[2] = fpair[2:3, :] - (two_pi / (NBLK * DEPTH)) * long_z
 
     landed(e_p.at[1:], ep_r)
     esum = e_p[0]
     for s in range(1, XS * ys):
         esum = esum + e_p[s]
     etot = 0.5 * jnp.sum(elong, axis=0, keepdims=True) + esum
-    energy_ref[0, 0] = jnp.sum(etot) * (1.0 / (cols_x * cols_y * ATOMS))
+    etot = jnp.sum(etot, axis=1, keepdims=True) * (1.0 / (cols_x * cols_y * ATOMS))
+    out_ref[3] = jnp.broadcast_to(etot, (1, ATOMS))
     left(hood.at[0:8], halo_s)
     left(mine.at[0], rc_s)
     left(recv_p.at[1:], rp_s)
@@ -496,7 +481,6 @@
     left(full.at[core], gc_s)
     left(e_z.at[1:], ez_s)
     left(e_p.at[1:], ep_s)
-    left(e_c.at[core], ec_s)
 
 
 def column(sizes, positions, features, nbr_tiles, kvec_index, weight_charge, weight_pair):
@@ -512,7 +496,7 @@
         vmem((3, KVEC), jnp.int32),
         vmem((QCH, 128), BF16),
         vmem((PCH, 128), BF16),
-        vmem((9, PCH + 8, ATOMS), F32),
+        vmem((9, PCH + 3, ATOMS), F32),
         vmem((CORES, XS, PART, TILE), F32),
         vmem((XS, PART, TILE), F32),
         vmem((PART, TILE), F32),
@@ -521,18 +505,13 @@
         vmem((zs, sub, TILE), F32),
         vmem((ps, sub, TILE), F32),
         vmem((CORES, XS, PART, TILE), F32),
-        vmem((zs, 1, TILE), F32),
+        vmem((CORES * zs, 1, TILE), F32),
         vmem((ps, 1, TILE), F32),
-        vmem((CORES, 1, TILE), F32),
         vmem((PADDED, ATOMS), F32),
         vmem((PADDED, ATOMS), BF16),
-        vmem((PADDED, ATOMS), BF16),
-        vmem((2 * TILE, ATOMS), F32),
+        vmem((CORES, TILE, ATOMS), F32),
         vmem((2 * TILE, ATOMS), BF16),
-        vmem((2 * TILE, ATOMS), BF16),
-        vmem((PADDED, 768), F32),
-        vmem((PADDED, 768), BF16),
-        vmem((PADDED, 768), BF16),
+        vmem((PADDED, 3 * TILE), F32),
         vmem((2, PAIRS, TILE), F32),
         vmem((8, KVEC), jnp.int32),
         vmem((ATOMS, 3 * PCH), BF16),
@@ -545,16 +524,13 @@
         dma((6,)),
     ]
     one, each_x = dma(()), dma((XS,))
-    scratch += [one, one, one, each_x, one, one, one, one, one, each_x, one, one, one, one, one, one, one, one]
+    scratch += [one, one, one, one, one, each_x, one, one, one, one, one, each_x, one, one, one, one, one, one]
     anywhere = pl.BlockSpec(memory_space=pl.ANY)
-    energy, forces = pl.pallas_call(
+    out = pl.pallas_call(
         functools.partial(kernel, sizes),
-        out_shape=(
-            jax.ShapeDtypeStruct((1, 1), F32),
-            pltpu.VMEM((3, 1, ATOMS), F32),
-        ),
+        out_shape=pltpu.VMEM((4, 1, ATOMS), F32),
         in_specs=[anywhere] * 6,
-        out_specs=(pl.BlockSpec(memory_space=pltpu.SMEM), pl.BlockSpec(memory_space=pltpu.VMEM)),
+        out_specs=pl.BlockSpec(memory_space=pltpu.VMEM),
         scratch_shapes=scratch,
         compiler_params=pltpu.CompilerParams(
             collective_id=0, has_side_effects=True, vmem_limit_bytes=60 * 1024 * 1024
@@ -567,7 +543,7 @@
         weight_charge,
         weight_pair,
     )
-    return energy[0, 0], forces.reshape(1, 1, 3, ATOMS)
+    return out[3, 0, 0], out[:3].reshape(1, 1, 3, ATOMS)
 
 
 def solution(mesh):

time: 42.9 us -> 39.1 us (0.911)
  Pallas kernels: 39.8 us -> 37.2 us
  between operations: 2.33 us -> 0.64 us
  local copies, waits for them, and re-layouts: 0.6 us -> 1.11 us
    pallas_call x1, Pallas kernels: 39.8 us -> 37.2 us  [column(): pl.pallas_call(functools.partial(kernel, sizes), out_shape=pltpu.VMEM((4,...]
    slice x0 -> x1, local copies, waits for them, and re-layouts: none -> 0.51 us  [column(): return (out[3, 0, 0], out[:3].reshape(1, 1, 3, ATOMS))]
where the time goes in v4:
time: 39.1 us; the launch traced here: 38.9 us
  Pallas kernels  37.2 us (95%)
  local copies, waits for them, and re-layouts  1.11 us (3%)
  between operations  0.64 us (2%)
    pallas_call x1, Pallas kernels, column(): pl.pallas_call(functools.partial(kernel, sizes), out_shape=pltpu.VMEM((4,...  37.2 us

profile of v4, /device:TPU:1, one launch (start us, length us, event | category | flops | bytes accessed | tf_op | source)
XLA Modules:
  0.0 38.9 jit_solution(16075370165262314090)
XLA Ops:
  0.6 37.2 %shard_map.77 = f32[4,1,384]{2,1,0:T(1,128)S(1)} custom-call(f32[3,1,384]{2,1,0:T(1,128)} %bitcast.9, bf16[128,384]{1,0:T(8,128)(2,1)} %bitcast.8, s32[3,1,32]{2,1,0:T(1,128)} %bitcast.10, s32[3,4096]{1,0:T(4,128)} %kidx_hbm.1, bf16[16,128]{1,0:T(8,128)(2,1)} %wc_hbm.1, bf16[16,128]{1,0:T(8,128)(2,1)} %wp_hbm.1), custom_call_target="tpu_custom_call" | custom-call | tf_op jit(solution)/shard_map/pallas_call | solution.py:529
  37.8 0.5 %slice.6 = f32[1,1,1]{2,1,0:T(1,128)} slice(f32[4,1,384]{2,1,0:T(1,128)S(1)} %shard_map.77), slice={[3:4], [0:1], [0:1]} | slice | bytes 8 | tf_op jit(solution)/shard_map/slice | solution.py:546
  38.3 0.6 %slice_bitcast_fusion = f32[1,1,3,384]{3,1,2,0:T(1,128)} fusion(f32[4,1,384]{2,1,0:T(1,128)S(1)} %shard_map.77), kind=kLoop, calls=%fused_computation | loop fusion | bytes 9216

commit v5 on v4

--- a/solution.py
+++ b/solution.py
@@ -229,13 +229,13 @@
         mine[1, j] = part[:, TILE:]
 
     pl.semaphore_wait(barrier, len(partners))
-    for j in rotated:
-        copy(mine.at[other, j], recv_c.at[j], rc_s, rc_r.at[j], core_dev).start()
     for ix, iy in halo:
         k = 3 * ix + iy
         copy(hood.at[4], hood.at[k], halo_s, halo_x if iy == 1 else halo_y, halo_dev(ix, iy)).start()
 
 
+    for j in rotated:
+        copy(mine.at[other, j], recv_c.at[j], rc_s, rc_r.at[j], core_dev).start()
     for j in rotated:
         landed(recv_c.at[j], rc_r.at[j])
         acc_x[...] = mine[core, j] + recv_c[j]
@@ -269,7 +269,7 @@
         fj = jnp.concatenate([high, high, low], axis=0)
         mbuf[slot] = jnp.dot(fi[...], fj, preferred_element_type=F32)
 
-    def pair_column(k, slot):
+    def pair_column(k, slot, energy=True, force=True):
         shift_x = (lax.div(k, 3) - 1).astype(F32) * (WIDTH / CUT)
         shift_y = (lax.rem(k, 3) - 1).astype(F32) * (WIDTH / CUT)
         xj = hood[k, PCH : PCH + 1, :] + shift_x
@@ -281,7 +281,8 @@
             for g in range(TILE // 32):
                 rows = slice(b * TILE + 32 * g, b * TILE + 32 * g + 32)
                 xi, yi, zi = pi[0, rows, :], pi[1, rows, :], pi[2, rows, :]
-                ax, ay, az = acc_p[0, rows, :], acc_p[1, rows, :], acc_p[2, rows, :]
+                if force:
+                    ax, ay, az = acc_p[0, rows, :], acc_p[1, rows, :], acc_p[2, rows, :]
                 for c in range(NBLK):
                     cols = slice(c * TILE, (c + 1) * TILE)
                     zc = zj[:, cols]
@@ -293,35 +294,38 @@
                     dx, dy, dz = xi - xj[:, cols], yi - yj[:, cols], zi - zc
                     w = jnp.maximum(limit - (dx * dx + dy * dy + dz * dz), 0.0)
                     mw = mbuf[slot, rows, cols] * w
-                    ax = ax + mw * dx
-                    ay = ay + mw * dy
-                    az = az + mw * dz
-                    ae = ae + mw * w
-                acc_p[0, rows, :] = ax
-                acc_p[1, rows, :] = ay
-                acc_p[2, rows, :] = az
-        acc_e[...] = ae
-
-    couple(4, 0)
-    pair_column(jnp.int32(4), 0)
+                    if force:
+                        ax = ax + mw * dx
+                        ay = ay + mw * dy
+                        az = az + mw * dz
+                    if energy:
+                        ae = ae + mw * w
+                if force:
+                    acc_p[0, rows, :] = ax
+                    acc_p[1, rows, :] = ay
+                    acc_p[2, rows, :] = az
+        if energy:
+            acc_e[...] = ae
 
     landed(hood.at[0:2], halo_x)
     for ix in (0, 2):
         for iy in (0, 2):
             copy(hood.at[3 * ix + 1], hood.at[3 * ix + iy], halo_s, halo_d, halo_dev(1, iy)).start()
+    couple(4, 0)
+    pair_column(jnp.int32(4), 0)
     landed(hood.at[0:2], halo_y)
 
-    def pair_columns(column_of):
+    def pair_columns(column_of, **parts):
         couple(column_of(0), 0)
 
         def pair_step(i, carry):
             slot = lax.rem(i, 2)
             couple(column_of(i + 1), 1 - slot)
-            pair_column(column_of(i), slot)
+            pair_column(column_of(i), slot, **parts)
             return carry
 
         lax.fori_loop(0, 3, pair_step, 0)
-        pair_column(jnp.int32(column_of(3)), 1)
+        pair_column(jnp.int32(column_of(3)), 1, **parts)
 
     pair_columns(lambda i: 2 * i + 1)
 
@@ -339,7 +343,11 @@
 
 
     landed(hood.at[0:4], halo_d)
-    pair_columns(lambda i: 2 * i + 2 * (i // 2) if isinstance(i, int) else 2 * i + 2 * lax.div(i, 2))
+
+    def corner(i):
+        return 2 * i + 2 * (i // 2 if isinstance(i, int) else lax.div(i, 2))
+
+    pair_columns(corner, force=False)
     own = jnp.sum(pair_feat * pair_feat, axis=0, keepdims=True)
     epart = jnp.sum(acc_e[...], axis=0, keepdims=True)
     for b in range(NBLK):
@@ -352,14 +360,6 @@
         copy(e_z.at[part], e_z.at[part], ez_s, ez_r, z_dev(j)).start()
         copy(e_z.at[part], e_z.at[part], ez_s, ez_r, z_dev(j, other)).start()
     copy(e_z.at[part], e_z.at[part], ez_s, ez_r, core_dev).start()
-    force_scale = 4.0 * SCALE / CUT
-    ones = jnp.ones((8, TILE), BF16)
-    for i in range(3):
-        high, low = split(acc_p[i])
-        sums = lax.dot_general(ones, high, (((1,), (1,)), ((), ())), preferred_element_type=F32)
-        sums = sums + lax.dot_general(ones, low, (((1,), (1,)), ((), ())), preferred_element_type=F32)
-        fpair[i : i + 1, :] = force_scale * sums[0:1]
-
     landed(recv_z.at[1:], rz_r)
     total = recv_z[0]
     for j in range(1, zs):
@@ -372,13 +372,6 @@
         def _(j=j, k=k):
             copy(gath_p.at[me], gath_p.at[me], gp_s, gp_r.at[x], plane_dev(j, k)).start()
 
-    landed(e_z.at[1:], ez_r)
-    esum = e_z[0]
-    for j in range(1, CORES * zs):
-        esum = esum + e_z[j]
-    e_p[me] = esum
-    for j, k in plane:
-        copy(e_p.at[me], e_p.at[me], ep_s, ep_r, plane_dev(j, k)).start()
     inputs[5].wait()
     kx, ky, kz = kidx_ref[0:1, :], kidx_ref[1:2, :], kidx_ref[2:3, :]
     codes[0:1, :] = kx * 17 + ky
@@ -417,7 +410,23 @@
     lanes = lax.broadcasted_iota(jnp.int32, (1, TILE), 1)
     coef[1] = jnp.where(lanes < 64, -green, green) * (cplus - cminus)
 
-    for j in x_order:
+    landed(e_z.at[1:], ez_r)
+    esum = e_z[0]
+    for j in range(1, CORES * zs):
+        esum = esum + e_z[j]
+    e_p[me] = esum
+    for j, k in plane:
+        copy(e_p.at[me], e_p.at[me], ep_s, ep_r, plane_dev(j, k)).start()
+    pair_columns(corner, energy=False)
+    force_scale = 4.0 * SCALE / CUT
+    ones = jnp.ones((8, TILE), BF16)
+    for i in range(3):
+        high, low = split(acc_p[i])
+        sums = lax.dot_general(ones, high, (((1,), (1,)), ((), ())), preferred_element_type=F32)
+        sums = sums + lax.dot_general(ones, low, (((1,), (1,)), ((), ())), preferred_element_type=F32)
+        fpair[i : i + 1, :] = force_scale * sums[0:1]
+
+    for j in [x_order[i] for i in (0, 1, 3, 2)]:
         landed(gath_p.at[pl.ds(j * ys, ys - 1 if j is x else ys)], gp_r.at[j])
         for k in range(ys):
             full[core, j, sub * k : sub * (k + 1), :] = gath_p[j * ys + k]

time: 39.1 us -> 38.8 us (level)
  no operation moved by 1% of the time
where the time goes in v5:
time: 38.8 us; the launch traced here: 38.7 us
  Pallas kernels  36.9 us (95%)
  local copies, waits for them, and re-layouts  1.11 us (3%)
  between operations  0.64 us (2%)
    pallas_call x1, Pallas kernels, column(): pl.pallas_call(functools.partial(kernel, sizes), out_shape=pltpu.VMEM((4,...  36.9 us

profile of v5, /device:TPU:1, one launch (start us, length us, event | category | flops | bytes accessed | tf_op | source)
XLA Modules:
  0.0 38.7 jit_solution(297280605318672563)
XLA Ops:
  0.6 36.9 %shard_map.77 = f32[4,1,384]{2,1,0:T(1,128)S(1)} custom-call(f32[3,1,384]{2,1,0:T(1,128)} %bitcast.9, bf16[128,384]{1,0:T(8,128)(2,1)} %bitcast.8, s32[3,1,32]{2,1,0:T(1,128)} %bitcast.10, s32[3,4096]{1,0:T(4,128)} %kidx_hbm.1, bf16[16,128]{1,0:T(8,128)(2,1)} %wc_hbm.1, bf16[16,128]{1,0:T(8,128)(2,1)} %wp_hbm.1), custom_call_target="tpu_custom_call" | custom-call | tf_op jit(solution)/shard_map/pallas_call | solution.py:538
  37.6 0.5 %slice.6 = f32[1,1,1]{2,1,0:T(1,128)} slice(f32[4,1,384]{2,1,0:T(1,128)S(1)} %shard_map.77), slice={[3:4], [0:1], [0:1]} | slice | bytes 8 | tf_op jit(solution)/shard_map/slice | solution.py:555
  38.1 0.6 %slice_bitcast_fusion = f32[1,1,3,384]{3,1,2,0:T(1,128)} fusion(f32[4,1,384]{2,1,0:T(1,128)S(1)} %shard_map.77), kind=kLoop, calls=%fused_computation | loop fusion | bytes 9216
